TPU v7x, 512 devices: a whole 4x4x16 slice. The times are simulated.
512 devices in a mesh: inst: 128 (over x, z, core), tp: 4 (over y).
Axes of the slice: x: 4, y: 4, z: 16, core: 2. Of those that a mesh axis runs over, the one named last changes fastest.
Arguments:
- query: bfloat16 [4, 256, 8192], P(None, 'inst', 'tp'), may hold values from -4.5 to 4.5
- fresh_key_value: bfloat16 [4, 256, 1024], P(None, 'inst', 'tp'), may hold values from -4.5 to 4.5
- kv_pool: bfloat16 [512, 2048, 1024], P('inst', None, 'tp'), may hold values from -4.5 to 4.5
- lengths: int32 [256], P('inst'), may hold values from 1 to 6144, as said below
- slot_owner: int32 [512], P(('inst', 'tp')), may hold values from 0 to 255, as said below
- slot_block: int32 [512], P(('inst', 'tp')), may hold values from 0 to 2, as said below
Outputs:
- attended: bfloat16 [4, 256, 8192], P(None, 'inst', 'tp')
Inputs may be any that keep to these rules, and one draw needn't show every extreme that they name: `slot_owner`: every instance owns exactly 4 blocks in the pools (request id // 2 is the owning instance), every request at least one; the 4 slots of one instance's pool belong to 4 different owning instances. `slot_block`: A request's blocks are numbered 0, 1, ... without gaps. `lengths`: A request with n blocks has between (n - 1) * 2048 + 1 and n * 2048 cached tokens.
All inputs are finite; a program needn't handle non-finite values.
Results may differ from a plain program's by a relative error of at most 0.0056.
Values may be sent and summed in bfloat16 or wider, within the bound.
A program may use at most 64 MiB of HBM per device.

v0:
```python
import math

import jax
import jax.numpy as jnp
from jax import lax
from jax.sharding import PartitionSpec as P


def partial_softmax(scores, valid, values, form):
    top = jnp.max(jnp.where(valid, scores, -jnp.inf), -1)
    weights = jnp.where(valid, jnp.exp(scores - top[..., None]), 0.0)
    total = jnp.sum(weights, -1)
    part = jnp.einsum(
        form, weights.astype(jnp.bfloat16), values, preferred_element_type=jnp.float32
    )
    return (part / total[..., None], top + jnp.log(total))


def shards(query, fresh_key_value, kv_pool, lengths, slot_owner, slot_block):
    steps, req_dev, width = query.shape
    slots, block, pair = kv_pool.shape
    head_width = pair // 2
    group = width // head_width
    me_inst = lax.axis_index("inst")
    scale = 1.0 / math.sqrt(head_width)
    owners_all, blocks_all = (
        lax.all_gather(slot_owner, ("inst", "tp"), axis=0, tiled=True),
        lax.all_gather(slot_block, ("inst", "tp"), axis=0, tiled=True),
    )
    lengths_all = lax.all_gather(lengths, "inst", axis=0, tiled=True)
    my_owner = lax.dynamic_slice_in_dim(owners_all, me_inst * slots, slots)
    my_block = lax.dynamic_slice_in_dim(blocks_all, me_inst * slots, slots)
    mine = jnp.arange(req_dev, dtype=jnp.int32) + me_inst * req_dev
    gathered = lax.all_gather(query, "inst", axis=1, tiled=True)
    pick = (my_owner[:, None] == jnp.arange(gathered.shape[1], dtype=jnp.int32)[None, :]).astype(
        jnp.bfloat16
    )
    chosen = jnp.einsum("sr,arw->saw", pick, gathered, preferred_element_type=jnp.float32).astype(
        jnp.bfloat16
    )
    q_rows = chosen.reshape(slots, steps * group, head_width)
    scores = (
        jnp.einsum(
            "sgd,std->sgt", q_rows, kv_pool[:, :, :head_width], preferred_element_type=jnp.float32
        )
        * scale
    )
    slot_len = jnp.take(lengths_all, my_owner)
    valid = (
        my_block[:, None] * block + jnp.arange(block, dtype=jnp.int32)[None, :] < slot_len[:, None]
    )
    part, part_lse = partial_softmax(
        scores, valid[:, None, :], kv_pool[:, :, head_width:], "sgt,std->sgd"
    )
    part_rows = part.astype(jnp.bfloat16)
    lse_all = lax.all_gather(part_lse, "inst", axis=0, tiled=True)
    query_tail = query.reshape(steps, req_dev, group, head_width)
    tail_score_rows = (
        jnp.einsum(
            "nhle,zhe->hnlz",
            query_tail,
            fresh_key_value[:, :, :head_width],
            preferred_element_type=jnp.float32,
        )
        * scale
    )
    steps_idx = jnp.arange(steps, dtype=jnp.int32)
    causal_mask = (steps_idx[:, None] >= steps_idx[None, :])[None, :, None, :]
    tail_part, tail_lse = partial_softmax(
        tail_score_rows, causal_mask, fresh_key_value[:, :, head_width:], "ksot,tkr->ksor"
    )
    tail_part = tail_part.reshape(req_dev, steps * group, head_width)
    tail_lse = tail_lse.reshape(req_dev, steps * group)
    peak = tail_lse
    numer = tail_part
    denom = jnp.ones_like(tail_lse)
    hit = owners_all[:, None] == mine[None, :]
    masked = jnp.where(hit[:, :, None], lse_all[:, None, :], -jnp.inf)
    new_peak = jnp.maximum(peak, jnp.max(masked, 0))
    shrink_factor = jnp.exp(peak - new_peak)
    scaled = jnp.exp(masked - new_peak[None])
    added = jnp.einsum(
        "nqg,ngd->qgd",
        scaled,
        lax.all_gather(part_rows, "inst", axis=0, tiled=True).astype(jnp.float32),
        precision=lax.Precision.HIGHEST,
    )
    peak, numer, denom = (
        new_peak,
        numer * shrink_factor[..., None] + added,
        denom * shrink_factor + jnp.sum(scaled, 0),
    )
    final = (numer / denom[..., None]).reshape(req_dev, steps, group, head_width)
    return jnp.transpose(final, (1, 0, 2, 3)).reshape(steps, req_dev, width).astype(jnp.bfloat16)


def solution(mesh):
    placed = (
        P(None, "inst", "tp"),
        P(None, "inst", "tp"),
        P("inst", None, "tp"),
        P("inst"),
        P(("inst", "tp")),
        P(("inst", "tp")),
    )
    return jax.shard_map(
        shards, mesh=mesh, in_specs=placed, out_specs=P(None, "inst", "tp"), check_vma=False
    )
```

profile of v0, /device:TPU:24, one launch (start us, length us, event | category | flops | bytes accessed | tf_op | source)
XLA Modules:
  0.0 332.4 jit_solution(9742797282177942107)
XLA Ops:
  6.5 1.4 copy.43
  9.3 1.3 dynamic-slice
  10.6 0.1 dynamic-update-slice
  10.7 0.1 dynamic-update-slice.1
  11.4 0.9 dynamic-update-slice.2
  12.3 34.4 %all-reduce.2 = s32[256]{0:T(256)S(1)} all-reduce(s32[256]{0:T(256)S(1)} %dynamic-update-slice.2), channel_id=1, replica_groups=mesh['inst'=128,'tp'=4] {'inst'}, use_global_device_ids=true, to_apply=%add.2 | all-reduce | flops 256 | bytes 2048
  46.6 98.5 %all-reduce.3 = (s32[512]{0:T(512)S(1)}, s32[512]{0:T(512)S(1)}) all-reduce(s32[512]{0:T(512)S(1)} %dynamic-update-slice, s32[512]{0:T(512)S(1)} %dynamic-update-slice.1), channel_id=1, replica_groups=mesh['inst'=128,'tp'=4] {'inst','tp'}, use_global_device_ids=true, to_apply=%add | all-reduce | flops 1024 | bytes 8192
  145.2 0.6 gather_fusion
  146.0 10.9 %all-gather.4.cloned.1.call-done = bf16[4,256,2048]{2,0,1:T(4,128)(2,1)} async-done(((bf16[4,2,2048]{2,0,1:T(4,128)(2,1)}), bf16[4,256,2048]{2,0,1:T(4,128)(2,1)}) %all-gather.4.cloned.1.call-update) | async-done | bytes 4194320 | tf_op jit(solution)/shard_map/all_gather | solution.py:34
  156.9 6.6 %fusion.4 = bf16[4,4,2048]{2,0,1:T(4,128)(2,1)S(1)} fusion(bf16[4,256,2048]{2,0,1:T(4,128)(2,1)} %all-gather.4.cloned.1.call-done, s32[4]{0:T(128)S(1)} %get-tuple-element.10), kind=kOutput, calls=%fused_computation.6 | convolution fusion | flops 16811008 | bytes 4259856 | tf_op jit(solution)/shard_map/sr,arw->saw/dot_general | solution.py:38
  163.6 2.7 select_reduce_fusion
  166.3 0.6 fusion.11
  166.9 1.2 fusion.15
  168.2 0.2 select_reduce_fusion.2
  168.7 0.3 convolution_divide_fusion
  169.0 98.8 %all-gather = f32[128,4,64]{2,1,0:T(4,128)S(1)} all-gather(f32[1,4,64]{2,1,0:T(4,128)S(1)} %add_bitcast_fusion), channel_id=1, replica_groups=mesh['inst'=128,'tp'=4] {'inst'}, dimensions={0}, use_global_device_ids=true | all-gather | bytes 132096 | tf_op jit(solution)/shard_map/all_gather | solution.py:56
  267.8 0.1 copy.46
  267.9 0.2 select_reduce_fusion.1
  268.2 0.1 copy.50
  268.3 0.3 fusion.35
  268.7 0.1 copy.48
  268.8 0.1 copy.53
  268.9 42.7 %all-gather.6.cloned.1.call-done = bf16[512,64,128]{2,1,0:T(8,128)(2,1)} async-done(((bf16[4,64,128]{2,1,0:T(8,128)(2,1)}), bf16[512,64,128]{2,1,0:T(8,128)(2,1)}) %all-gather.6.cloned.1.call-update) | async-done | bytes 8388624 | tf_op jit(solution)/shard_map/all_gather | solution.py:85
  311.6 13.9 %fusion.31 = bf16[2,64,128]{2,0,1:T(2,128)(2,1)} fusion(bf16[512,64,128]{2,1,0:T(8,128)(2,1)} %all-gather.6.cloned.1.call-done, pred[512,2]{0,1:T(4,128)(4,1)S(1)} %broadcast_compare_fusion, f32[2,64]{0,1:T(8,128)S(1)} %copy.50, f32[512,64]{0,1:T(8,128)S(1)} %copy.46, f32[2,64,128]{2,1,0:T(8,128)S(1)} %bitcast.41, f32[2,64]{0,1:T(8,128)S(1)} %copy.53, ...), kind=kOutput, calls=%fused_computation.24 | convolution fusion | flops 100859904 | bytes 8620544 | tf_op jit(solution)/shard_map/nqg,ngd->qgd/dot_general | solution.py:82
  (32 shorter events, 0.8 us)
Async XLA Ops:
  6.5 150.3 %all-gather.4.cloned.1.call-start = ((), (), s32[]{:S(2)}) async-start(), calls=%async_computation | async-start | bytes 4227072 | tf_op jit(solution)/shard_map/all_gather | solution.py:34
  8.0 303.7 %all-gather.6.cloned.1.call-start = ((), (), s32[]{:S(2)}) async-start(), calls=%async_computation.1 | async-start | bytes 8454144 | tf_op jit(solution)/shard_map/all_gather | solution.py:85
  163.6 3.3 copy-start
  166.9 1.2 copy-start.1
  166.9 1.3 copy-start.2
Sparse Core Ops, SparseCore 0:
  10.5 146.3 all-gather.3
  168.2 143.3 all-gather.5
where the time goes:
time: 334 us; the launch traced here: 332 us
  blocking collectives  232 us (69%)
  waiting for transfers between devices  53.6 us (16%)
  matrix products  24.9 us (7%)
  between operations  15.4 us (5%)
  local copies, waits for them, and re-layouts  5.16 us (2%)
    unnamed x2, blocking collectives  133 us
    all_gather x1, blocking collectives, shards(): lse_all = lax.all_gather(part_lse, 'inst', axis=0, tiled=True)  98.8 us
    all_gather x1, waiting for transfers between devices, shards(): lax.all_gather(part_rows, 'inst', axis=0, tiled=True).astype(jnp.float32)  42.7 us
    dot_general x1, matrix products, shards(): jnp.einsum('nqg,ngd->qgd', scaled, lax.all_gather(part_rows, 'inst', axis...  13.9 us
    all_gather x1, waiting for transfers between devices, shards(): gathered = lax.all_gather(query, 'inst', axis=1, tiled=True)  10.9 us
  transfers between devices with their start and end apart: 2, of which 2 were waited for; matrix products, arithmetic and copies ran while one was open for 2% of the time, Pallas kernels for 0%

commit v1 on v0

v1 whole, which is shorter than its diff:
```python
import math

import jax
import jax.numpy as jnp
from jax import lax
from jax.experimental import pallas as pl
from jax.experimental.pallas import tpu as pltpu
from jax.sharding import PartitionSpec as P

BLOCK = 2048
WIDTH = 128
ROWS = 64
NX, NZ, NC, NY = 4, 16, 2, 4
GROUPS = NX * NC
SLOTS = 4
SCALE = 1.0 / math.sqrt(WIDTH)
NEG = -1e30
F32 = jnp.float32
BF16 = jnp.bfloat16

HOPS = (6, -6, 2, -2)
NEXT = {6: (-1, 1, 2), -6: (1, -1), 2: (-1, 1, 2), -2: (1, -1, -2)}
FORWARD = [(d, f) for d in HOPS for f in NEXT[d]]
ROW_PEERS = [(dx, dc) for dx in range(NX) for dc in range(NC)][1:]


def kernel(
    q_ref, fresh_ref, kv_ref, len_ref, owner_ref, block_ref, out_ref,
    kv, qall, rowtab, ivec, tab_s, ivec_s, sel, got, parts, lses, lrow, wmat, wcol,
    cbuf, clse, rbuf, rlse, mbuf, mlse, fbuf, flse, tail, tail_lse,
    kv_sem, y_ss, y_rs, t_ss, t_rs, sm_sem, a_ss, a_rs, b_ss, b_rs, s_ss, s_rs,
    p_ss, p_rs, l_ss, l_rs, c_ss, c_rs, d_ss, d_rs, e_ss, e_rs, f_ss, f_rs,
):
    me = lax.axis_index("inst")
    y = lax.axis_index("tp")
    x, z, c = me // (NZ * NC), (me // NC) % NZ, me % NC
    g = x * NC + c

    def at(dx, dz, dc, dy):
        xx, zz = (x + dx + NX) % NX, (z + dz + NZ) % NZ
        cc, yy = (c + dc) % NC, (y + dy) % NY
        return ((xx * NZ + zz) * NC + cc, yy)

    def send(src, dst, ss, rs, to):
        return pltpu.make_async_remote_copy(
            src_ref=src, dst_ref=dst, send_sem=ss, recv_sem=rs,
            device_id=to, device_id_type=pl.DeviceIdType.MESH,
        )

    peers = [at(0, d, 0, 0) for d in (6, -6, 2, -2, 1, -1)]
    peers += [at(dx, 0, dc, 0) for dx, dc in ROW_PEERS]
    peers += [at(0, 0, 0, d) for d in range(1, NY)]
    barrier = pltpu.get_barrier_semaphore()
    for p in peers:
        pl.semaphore_signal(barrier, inc=1, device_id=p, device_id_type=pl.DeviceIdType.MESH)
    kv_copies = [pltpu.make_async_copy(kv_ref.at[s], kv.at[s], kv_sem.at[s]) for s in range(SLOTS)]
    for copy in kv_copies:
        copy.start()
    row = lax.broadcasted_iota(jnp.int32, (16, WIDTH), 0) % 4
    hi = jnp.where(row < 2, len_ref[0] // 64, len_ref[1] // 64)
    lo = jnp.where(row < 2, len_ref[0] % 64, len_ref[1] % 64)
    qall[z, 0:8] = q_ref[...]
    qall[z, 8] = jnp.where(row % 2 == 0, hi, lo).astype(F32).astype(BF16)
    rowtab[g, y] = jnp.full((1, WIDTH), owner_ref[0] * 4 + block_ref[0], jnp.int32)
    pl.semaphore_wait(barrier, len(peers))

    first = {
        d: send(qall.at[z], qall.at[z], a_ss.at[i], a_rs.at[i], at(0, d, 0, 0))
        for i, d in enumerate(HOPS)
    }
    for d in HOPS:
        first[d].start()
    tables = []
    for i in range(NY - 1):
        tables.append(send(rowtab.at[g, y], rowtab.at[g, y], y_ss.at[i], y_rs.at[i], at(0, 0, 0, i + 1)))
        tables[-1].start()

    for r in range(2):
        qf = q_ref[4 * r : 4 * r + 4].reshape(ROWS, WIDTH).astype(F32)
        step = lax.broadcasted_iota(jnp.int32, (ROWS, 1), 0) // 16
        ss = []
        for b in range(4):
            k_b = fresh_ref[b].astype(F32)[r : r + 1, :WIDTH]
            s_b = jnp.sum(qf * k_b, axis=1, keepdims=True) * SCALE
            ss.append(jnp.where(step >= b, s_b, -jnp.inf))
        top = jnp.maximum(jnp.maximum(ss[0], ss[1]), jnp.maximum(ss[2], ss[3]))
        ws = [jnp.exp(s_b - top) for s_b in ss]
        total = ws[0] + ws[1] + ws[2] + ws[3]
        acc = jnp.zeros((ROWS, WIDTH), F32)
        for b in range(4):
            v_b = fresh_ref[b].astype(F32)[r : r + 1, WIDTH:]
            acc = acc + ws[b].astype(BF16).astype(F32) * v_b
        tail[r] = acc / total
        tail_lse[r] = jnp.broadcast_to(top + jnp.log(total), (ROWS, WIDTH))

    for t in tables:
        t.wait_recv()
    rows = []
    for i, (dx, dc) in enumerate(ROW_PEERS):
        rows.append(send(rowtab.at[g], rowtab.at[g], t_ss.at[i], t_rs.at[i], at(dx, 0, dc, 0)))
        rows[-1].start()

    second = []
    for d in (2, -2, 6, -6):
        first[d].wait_recv()
        came = (z - d + NZ) % NZ
        for j, (dd, f) in enumerate(FORWARD):
            if dd == d:
                second.append(send(qall.at[came], qall.at[came], b_ss.at[j], b_rs.at[j], at(0, f, 0, 0)))
                second[-1].start()

    for t in rows:
        t.wait_recv()
    lane = lax.broadcasted_iota(jnp.int32, (1, WIDTH), 1)
    want = (((x * NZ + (lane % 32) // 2) * NC + c) * 2 + lane % 2) * 4 + lane // 32
    index = jnp.zeros((1, WIDTH), jnp.int32)
    count = jnp.zeros((1, WIDTH), jnp.int32)
    for gg in range(GROUPS):
        for s in range(SLOTS):
            hit = rowtab[gg, s] == want
            index = jnp.where(hit, gg * SLOTS + s, index)
            count = jnp.where(hit, 1, count)
    ivec[0] = index
    ivec[1] = count
    to_smem = [
        pltpu.make_async_copy(rowtab, tab_s, sm_sem.at[0]),
        pltpu.make_async_copy(ivec, ivec_s, sm_sem.at[1]),
    ]
    for copy in to_smem:
        copy.start()
    for copy in to_smem:
        copy.wait()

    for t in second:
        t.wait_recv()

    group = lax.broadcasted_iota(jnp.int32, (16, WIDTH), 0) // 4

    def choose(gg, put):
        lens = jnp.zeros((16, WIDTH), BF16)
        for s in range(SLOTS):
            owner = tab_s[gg, s, 0, 0] // 4
            zz, r = (owner // 4) % NZ, owner % 2
            put(slice(4 * s, 4 * s + 4), qall[zz, pl.ds(4 * r, 4)])
            lens = jnp.where(group == s, qall[zz, 8].astype(F32), lens.astype(F32)).astype(BF16)
        put(16, lens)

    queries = []
    for i, (dx, dc) in enumerate(ROW_PEERS):
        gg = ((x + dx) % NX) * NC + (c + dc) % NC

        def put(k, v, i=i):
            sel[i, k] = v

        choose(gg, put)
        queries.append(send(sel.at[i], got.at[g], s_ss.at[i], s_rs.at[i], at(dx, 0, dc, 0)))
        queries[-1].start()

    def put_own(k, v):
        got[g, k] = v

    choose(g, put_own)
    for copy in kv_copies:
        copy.wait()
    for t in queries:
        t.wait_recv()

    lane_pos = lax.broadcasted_iota(jnp.int32, (1, BLOCK), 1).astype(F32)
    lane_id = lax.broadcasted_iota(jnp.int32, (ROWS, WIDTH), 1)
    lcols = jnp.zeros((ROWS, WIDTH), F32)
    back = []
    for s in range(SLOTS):
        code = tab_s[g, s, 0, 0]
        owner, blk = code // 4, code % 4
        src = (owner // 64) * NC + (owner // 2) % NC
        r = owner % 2
        q = got[src, pl.ds(4 * s, 4)].reshape(ROWS, WIDTH)
        lens = got[src, 16].astype(F32)
        hi = jnp.where(r == 0, lens[4 * s : 4 * s + 1], lens[4 * s + 2 : 4 * s + 3])
        lo = jnp.where(r == 0, lens[4 * s + 1 : 4 * s + 2], lens[4 * s + 3 : 4 * s + 4])
        left = (hi * 64.0 + lo)[:, :1] - (blk * BLOCK).astype(F32)
        scores = lax.dot_general(
            q, kv[s, :, :WIDTH], (((1,), (1,)), ((), ())), preferred_element_type=F32
        ) * SCALE
        scores = jnp.where(lane_pos < left, scores, -jnp.inf)
        top = jnp.max(scores, axis=1, keepdims=True)
        weights = jnp.exp(scores - top)
        total = jnp.sum(weights, axis=1, keepdims=True)
        part = jnp.dot(weights.astype(BF16), kv[s, :, WIDTH:], preferred_element_type=F32) / total
        parts[g, s] = part.astype(BF16).reshape(4, 16, WIDTH)
        lcols = jnp.where(lane_id == s, top + jnp.log(total), lcols)
        for i, (dx, dc) in enumerate(ROW_PEERS):
            copy = send(parts.at[g, s], parts.at[g, s], p_ss.at[i, s], p_rs.at[i, s], at(dx, 0, dc, 0))
            copy.start()
            back.append(copy)
    lt = jnp.concatenate([lcols, lcols], axis=0).T
    for s in range(SLOTS):
        lses[g, s] = lt[s : s + 1]
    for i, (dx, dc) in enumerate(ROW_PEERS):
        copy = send(lses.at[g], lses.at[g], l_ss.at[i], l_rs.at[i], at(dx, 0, dc, 0))
        copy.start()
        back.append(copy)
    for copy in back:
        copy.wait_recv()

    half = lax.broadcasted_iota(jnp.int32, (1, WIDTH), 1) < ROWS
    wmat[...] = jnp.zeros((WIDTH, WIDTH), F32)

    def where_is(d, r, k):
        j = k * 32 + ((z + d) % NZ) * 2 + r
        return ivec_s[0, 0, j], ivec_s[1, 0, j]

    for d in range(NZ):
        for k in range(3):
            pair = []
            for r in range(2):
                i, n = where_is(d, r, k)
                pair.append(jnp.where(n > 0, lses[i // 4, i % 4], NEG))
            lrow[k, d] = jnp.where(half, pair[0], pair[1])[0]
    l0, l1, l2 = lrow[0], lrow[1], lrow[2]
    peak = jnp.maximum(jnp.maximum(l0, l1), l2)
    w0, w1, w2 = jnp.exp(l0 - peak), jnp.exp(l1 - peak), jnp.exp(l2 - peak)
    total = w0 + w1 + w2
    merged = peak + jnp.log(total)
    wmat[0:16] = w0 / total
    wmat[16:32] = w1 / total
    wmat[32:48] = w2 / total
    for d in range(NZ):
        clse[d] = merged[d : d + 1]
    wcol[...] = wmat[...].T

    def build(d):
        d = d % NZ
        for r in range(2):
            acc = jnp.zeros((ROWS, WIDTH), F32)
            for k in range(3):
                i, _ = where_is(d, r, k)
                p = parts[i // 4, i % 4].reshape(ROWS, WIDTH).astype(F32)
                acc = acc + wcol[r * ROWS : (r + 1) * ROWS, k * 16 + d : k * 16 + d + 1] * p
            cbuf[d, 4 * r : 4 * r + 4] = acc.astype(BF16).reshape(4, 16, WIDTH)

    relayed = []
    for j, (dd, f) in enumerate(FORWARD):
        e = (-f - dd) % NZ
        build(e)
        relayed.append(
            (
                send(cbuf.at[e], rbuf.at[j], c_ss.at[j], c_rs.at[j], at(0, -f, 0, 0)),
                send(clse.at[e], rlse.at[j], d_ss.at[j], d_rs.at[j], at(0, -f, 0, 0)),
            )
        )
        for copy in relayed[-1]:
            copy.start()
    for d in HOPS:
        build(-d)
    build(0)
    final = []
    for i, d in enumerate(HOPS):
        js = [j for j, (dd, _) in enumerate(FORWARD) if dd == d]
        for j in js:
            for copy in relayed[j]:
                copy.wait_recv()
        ls = [clse[(-d) % NZ]] + [rlse[j] for j in js]
        peak = ls[0]
        for l in ls[1:]:
            peak = jnp.maximum(peak, l)
        ws = [jnp.exp(l - peak) for l in ls]
        total = ws[0]
        for w in ws[1:]:
            total = total + w
        mlse[i] = peak + jnp.log(total)
        for n, w in enumerate(ws):
            wmat[n : n + 1] = w / total
        wt = wmat[...].T
        data = [cbuf[(-d) % NZ]] + [rbuf[j] for j in js]
        acc = jnp.zeros((WIDTH, WIDTH), F32)
        for n, p in enumerate(data):
            acc = acc + wt[:, n : n + 1] * p.reshape(WIDTH, WIDTH).astype(F32)
        mbuf[i] = acc.astype(BF16).reshape(8, 16, WIDTH)
        final.append(
            (
                send(mbuf.at[i], fbuf.at[i], e_ss.at[i], e_rs.at[i], at(0, -d, 0, 0)),
                send(mlse.at[i], flse.at[i], f_ss.at[i], f_rs.at[i], at(0, -d, 0, 0)),
            )
        )
        for copy in final[-1]:
            copy.start()
    for pair in final:
        for copy in pair:
            copy.wait_recv()
    for i in range(4):
        wmat[i : i + 1] = flse[i]
    wmat[4:5] = clse[0]
    wt = wmat[...].T
    for r in range(2):
        rs = slice(r * ROWS, (r + 1) * ROWS)
        tl = tail_lse[r][:, :1]
        ls = [wt[rs, n : n + 1] for n in range(5)]
        peak = tl
        for l in ls:
            peak = jnp.maximum(peak, l)
        w = jnp.exp(tl - peak)
        denom = w
        acc = w * tail[r]
        for n in range(5):
            p = cbuf[0, 4 * r : 4 * r + 4] if n == 4 else fbuf[n, 4 * r : 4 * r + 4]
            w = jnp.exp(ls[n] - peak)
            denom = denom + w
            acc = acc + w * p.reshape(ROWS, WIDTH).astype(F32)
        out_ref[4 * r : 4 * r + 4] = (acc / denom).astype(BF16).reshape(4, 16, WIDTH)

    for copy in list(first.values()) + tables + rows + second + queries + back:
        copy.wait_send()
    for pair in relayed + final:
        for copy in pair:
            copy.wait_send()


def shards(query, fresh_key_value, kv_pool, lengths, slot_owner, slot_block):
    steps, req_dev, width = query.shape
    q = jnp.transpose(query.reshape(steps, req_dev, 16, WIDTH), (1, 0, 2, 3)).reshape(8, 16, WIDTH)
    dma = pltpu.SemaphoreType.DMA
    vmem, smem = pl.BlockSpec(memory_space=pltpu.VMEM), pl.BlockSpec(memory_space=pltpu.SMEM)
    n, m = len(ROW_PEERS), len(FORWARD)
    out = pl.pallas_call(
        kernel,
        out_shape=jax.ShapeDtypeStruct((8, 16, WIDTH), BF16),
        in_specs=[vmem, vmem, pl.BlockSpec(memory_space=pl.ANY), smem, smem, smem],
        out_specs=vmem,
        scratch_shapes=[
            pltpu.VMEM((SLOTS, BLOCK, 2 * WIDTH), BF16),
            pltpu.VMEM((NZ, 9, 16, WIDTH), BF16),
            pltpu.VMEM((GROUPS, SLOTS, 1, WIDTH), jnp.int32),
            pltpu.VMEM((2, 1, WIDTH), jnp.int32),
            pltpu.SMEM((GROUPS, SLOTS, 1, WIDTH), jnp.int32),
            pltpu.SMEM((2, 1, WIDTH), jnp.int32),
            pltpu.VMEM((n, 17, 16, WIDTH), BF16),
            pltpu.VMEM((GROUPS, 17, 16, WIDTH), BF16),
            pltpu.VMEM((GROUPS, SLOTS, 4, 16, WIDTH), BF16),
            pltpu.VMEM((GROUPS, SLOTS, 1, WIDTH), F32),
            pltpu.VMEM((3, NZ, WIDTH), F32),
            pltpu.VMEM((WIDTH, WIDTH), F32),
            pltpu.VMEM((WIDTH, WIDTH), F32),
            pltpu.VMEM((NZ, 8, 16, WIDTH), BF16),
            pltpu.VMEM((NZ, 1, WIDTH), F32),
            pltpu.VMEM((m, 8, 16, WIDTH), BF16),
            pltpu.VMEM((m, 1, WIDTH), F32),
            pltpu.VMEM((4, 8, 16, WIDTH), BF16),
            pltpu.VMEM((4, 1, WIDTH), F32),
            pltpu.VMEM((4, 8, 16, WIDTH), BF16),
            pltpu.VMEM((4, 1, WIDTH), F32),
            pltpu.VMEM((2, ROWS, WIDTH), F32),
            pltpu.VMEM((2, ROWS, WIDTH), F32),
            dma((SLOTS,)),
            dma((3,)), dma((3,)),
            dma((n,)), dma((n,)),
            dma((2,)),
            dma((4,)), dma((4,)),
            dma((m,)), dma((m,)),
            dma((n,)), dma((n,)),
            dma((n, SLOTS)), dma((n, SLOTS)),
            dma((n,)), dma((n,)),
            dma((m,)), dma((m,)),
            dma((m,)), dma((m,)),
            dma((4,)), dma((4,)),
            dma((4,)), dma((4,)),
        ],
        compiler_params=pltpu.CompilerParams(
            collective_id=0, has_side_effects=True, vmem_limit_bytes=40 << 20
        ),
        name="lent_attention",
    )(q, fresh_key_value, kv_pool, lengths, slot_owner, slot_block)
    out = jnp.transpose(out.reshape(req_dev, steps, 16, WIDTH), (1, 0, 2, 3))
    return out.reshape(steps, req_dev, width)


def solution(mesh):
    placed = (
        P(None, "inst", "tp"),
        P(None, "inst", "tp"),
        P("inst", None, "tp"),
        P("inst"),
        P(("inst", "tp")),
        P(("inst", "tp")),
    )
    return jax.shard_map(
        shards, mesh=mesh, in_specs=placed, out_specs=P(None, "inst", "tp"), check_vma=False
    )
```

time: 334 us -> 74.5 us (0.22)
  the two profiles are of different devices: /device:TPU:24 before, /device:TPU:8 now
where the time goes in v1:
time: 74.5 us; the launch traced here: 74.2 us
  Pallas kernels  67.9 us (91%)
  local copies, waits for them, and re-layouts  4.98 us (7%)
  between operations  1.33 us (2%)
    pallas_call x1, Pallas kernels, shards(): pl.pallas_call(kernel, out_shape=jax.ShapeDtypeStruct((8, 16, WIDTH), BF1...  67.9 us
    unnamed x6, local copies, waits for them, and re-layouts  3.52 us

profile of v1, /device:TPU:8, one launch (start us, length us, event | category | flops | bytes accessed | tf_op | source)
XLA Modules:
  0.0 74.2 jit_solution(11649679228930336951)
XLA Ops:
  1.3 0.8 %reshape.12 = bf16[4,2,16,128]{3,2,1,0:T(8,128)(2,1)S(1)} reshape(bf16[4,2,2048]{2,1,0:T(2,128)(2,1)} %param.6) | data formatting | bytes 65536 | tf_op jit(solution)/shard_map/reshape | solution.py:321
  2.1 0.0 copy-start
  2.1 2.2 %copy-done = bf16[4,2048,256]{2,1,0:T(8,128)(2,1)S(1)} copy-done((bf16[4,2048,256]{2,1,0:T(8,128)(2,1)S(1)}, bf16[4,2048,256]{2,1,0:T(8,128)(2,1)}, u32[]{:S(2)}) %copy-start) | copy-done | bytes 4194328
  4.3 0.0 copy-start.1
  4.3 0.7 copy-done.1
  5.0 0.0 copy-start.2
  5.0 0.7 copy-done.2
  5.6 67.9 %lent_attention.1 = bf16[8,16,128]{2,1,0:T(8,128)(2,1)S(1)} custom-call(bf16[8,16,128]{2,1,0:T(8,128)(2,1)S(1)} %bitcast.10, bf16[4,2,256]{2,1,0:T(2,128)(2,1)S(1)} %copy-done.1, bf16[4,2048,256]{2,1,0:T(8,128)(2,1)S(1)} %copy-done, s32[2]{0:T(128)S(1)} %copy-done.2, s32[1]{0:T(128)S(6)} %copy.10.owner_ref, s32[1]{0:T(128)S(6)} %copy.11.block_ref), custom_call_target="tpu_custom_call" | custom-call | tf_op jit(solution)/shard_map/lent_attention/pallas_call | solution.py:325
  73.6 0.6 copy.9
  (2 shorter events, 0.0 us)
Async XLA Ops:
  2.1 2.2 %copy-start = (bf16[4,2048,256]{2,1,0:T(8,128)(2,1)S(1)}, bf16[4,2048,256]{2,1,0:T(8,128)(2,1)}, u32[]{:S(2)}) copy-start(bf16[4,2048,256]{2,1,0:T(8,128)(2,1)} %kv_ref.1) | copy-start | bytes 12582916
  4.3 0.7 copy-start.1
  5.0 0.7 copy-start.2

commit v2 on v1

--- a/solution.py
+++ b/solution.py
@@ -18,18 +18,20 @@
 F32 = jnp.float32
 BF16 = jnp.bfloat16
 
-HOPS = (6, -6, 2, -2)
-NEXT = {6: (-1, 1, 2), -6: (1, -1), 2: (-1, 1, 2), -2: (1, -1, -2)}
+HOPS = (5, -5, 2, -2)
+NEXT = {5: (1, 2, 3), -5: (-1, -2), 2: (-1, 1, 2), -2: (1, -1, -2)}
 FORWARD = [(d, f) for d in HOPS for f in NEXT[d]]
 ROW_PEERS = [(dx, dc) for dx in range(NX) for dc in range(NC)][1:]
+GATHER = ((1, 0), (3, 0), (2, 0), (0, 1))
 
 
 def kernel(
-    q_ref, fresh_ref, kv_ref, len_ref, owner_ref, block_ref, out_ref,
-    kv, qall, rowtab, ivec, tab_s, ivec_s, sel, got, parts, lses, lrow, wmat, wcol,
+    q_in, fresh_in, kv_ref, len_in, owner_in, block_in, out_ref,
+    q_raw, q_ref, fresh_ref, len_ref, owner_ref, block_ref,
+    kv, qall, rowtab, ivec, tab_s, ivec_s, sel, got0, got1, parts, lses, lrow, wmat, wcol,
     cbuf, clse, rbuf, rlse, mbuf, mlse, fbuf, flse, tail, tail_lse,
-    kv_sem, y_ss, y_rs, t_ss, t_rs, sm_sem, a_ss, a_rs, b_ss, b_rs, s_ss, s_rs,
-    p_ss, p_rs, l_ss, l_rs, c_ss, c_rs, d_ss, d_rs, e_ss, e_rs, f_ss, f_rs,
+    in_sem, kv_sem, y_ss, y_rs, t_ss, t_rs, sm_sem, a_ss, a_rs, b_ss, b_rs, s_ss, s_rs,
+    p_ss, p_rs, l_ss, l_rs, u_ss, u_rs, v_ss, v_rs, c_ss, c_rs, d_ss, d_rs, e_ss, e_rs, f_ss, f_rs,
 ):
     me = lax.axis_index("inst")
     y = lax.axis_index("tp")
@@ -47,15 +49,30 @@
             device_id=to, device_id_type=pl.DeviceIdType.MESH,
         )
 
-    peers = [at(0, d, 0, 0) for d in (6, -6, 2, -2, 1, -1)]
+    peers = [at(0, d, 0, 0) for d in (5, -5, 3, -3, 2, -2, 1, -1)]
     peers += [at(dx, 0, dc, 0) for dx, dc in ROW_PEERS]
     peers += [at(0, 0, 0, d) for d in range(1, NY)]
     barrier = pltpu.get_barrier_semaphore()
     for p in peers:
         pl.semaphore_signal(barrier, inc=1, device_id=p, device_id_type=pl.DeviceIdType.MESH)
+    inputs = [
+        pltpu.make_async_copy(a, b, in_sem.at[i])
+        for i, (a, b) in enumerate(
+            ((q_in, q_raw), (len_in, len_ref), (owner_in, owner_ref), (block_in, block_ref), (fresh_in, fresh_ref))
+        )
+    ]
+    for copy in inputs:
+        copy.start()
     kv_copies = [pltpu.make_async_copy(kv_ref.at[s], kv.at[s], kv_sem.at[s]) for s in range(SLOTS)]
     for copy in kv_copies:
         copy.start()
+    for copy in inputs:
+        copy.wait()
+    for a in range(4):
+        qa = q_raw[a].astype(F32)
+        for r in range(2):
+            tile = jnp.concatenate([qa[r : r + 1, WIDTH * h : WIDTH * (h + 1)] for h in range(16)], axis=0)
+            q_ref[4 * r + a] = tile.astype(BF16)
     row = lax.broadcasted_iota(jnp.int32, (16, WIDTH), 0) % 4
     hi = jnp.where(row < 2, len_ref[0] // 64, len_ref[1] // 64)
     lo = jnp.where(row < 2, len_ref[0] % 64, len_ref[1] % 64)
@@ -101,7 +118,7 @@
         rows[-1].start()
 
     second = []
-    for d in (2, -2, 6, -6):
+    for d in (2, -2, 5, -5):
         first[d].wait_recv()
         came = (z - d + NZ) % NZ
         for j, (dd, f) in enumerate(FORWARD):
@@ -136,72 +153,92 @@
 
     group = lax.broadcasted_iota(jnp.int32, (16, WIDTH), 0) // 4
 
-    def choose(gg, put):
-        lens = jnp.zeros((16, WIDTH), BF16)
-        for s in range(SLOTS):
-            owner = tab_s[gg, s, 0, 0] // 4
+    got = (got0, got1)
+
+    def choose(gg, half, ref):
+        lens = jnp.zeros((16, WIDTH), F32)
+        for i in range(2):
+            owner = tab_s[gg, 2 * half + i, 0, 0] // 4
             zz, r = (owner // 4) % NZ, owner % 2
-            put(slice(4 * s, 4 * s + 4), qall[zz, pl.ds(4 * r, 4)])
-            lens = jnp.where(group == s, qall[zz, 8].astype(F32), lens.astype(F32)).astype(BF16)
-        put(16, lens)
+            ref[4 * i : 4 * i + 4] = qall[zz, pl.ds(4 * r, 4)]
+            lens = jnp.where(group == i, qall[zz, 8].astype(F32), lens)
+        ref[8] = lens.astype(BF16)
 
     queries = []
-    for i, (dx, dc) in enumerate(ROW_PEERS):
-        gg = ((x + dx) % NX) * NC + (c + dc) % NC
-
-        def put(k, v, i=i):
-            sel[i, k] = v
-
-        choose(gg, put)
-        queries.append(send(sel.at[i], got.at[g], s_ss.at[i], s_rs.at[i], at(dx, 0, dc, 0)))
-        queries[-1].start()
-
-    def put_own(k, v):
-        got[g, k] = v
-
-    choose(g, put_own)
+    for half in range(2):
+        for i, (dx, dc) in enumerate(ROW_PEERS):
+            gg = ((x + dx) % NX) * NC + (c + dc) % NC
+            choose(gg, half, sel.at[i, half])
+            copy = send(
+                sel.at[i, half], got[half].at[g], s_ss.at[i, half], s_rs.at[i, half], at(dx, 0, dc, 0)
+            )
+            copy.start()
+            queries.append(copy)
+        choose(g, half, got[half].at[g])
     for copy in kv_copies:
         copy.wait()
-    for t in queries:
-        t.wait_recv()
 
     lane_pos = lax.broadcasted_iota(jnp.int32, (1, BLOCK), 1).astype(F32)
     lane_id = lax.broadcasted_iota(jnp.int32, (ROWS, WIDTH), 1)
     lcols = jnp.zeros((ROWS, WIDTH), F32)
     back = []
-    for s in range(SLOTS):
-        code = tab_s[g, s, 0, 0]
-        owner, blk = code // 4, code % 4
-        src = (owner // 64) * NC + (owner // 2) % NC
-        r = owner % 2
-        q = got[src, pl.ds(4 * s, 4)].reshape(ROWS, WIDTH)
-        lens = got[src, 16].astype(F32)
-        hi = jnp.where(r == 0, lens[4 * s : 4 * s + 1], lens[4 * s + 2 : 4 * s + 3])
-        lo = jnp.where(r == 0, lens[4 * s + 1 : 4 * s + 2], lens[4 * s + 3 : 4 * s + 4])
-        left = (hi * 64.0 + lo)[:, :1] - (blk * BLOCK).astype(F32)
-        scores = lax.dot_general(
-            q, kv[s, :, :WIDTH], (((1,), (1,)), ((), ())), preferred_element_type=F32
-        ) * SCALE
-        scores = jnp.where(lane_pos < left, scores, -jnp.inf)
-        top = jnp.max(scores, axis=1, keepdims=True)
-        weights = jnp.exp(scores - top)
-        total = jnp.sum(weights, axis=1, keepdims=True)
-        part = jnp.dot(weights.astype(BF16), kv[s, :, WIDTH:], preferred_element_type=F32) / total
-        parts[g, s] = part.astype(BF16).reshape(4, 16, WIDTH)
-        lcols = jnp.where(lane_id == s, top + jnp.log(total), lcols)
-        for i, (dx, dc) in enumerate(ROW_PEERS):
-            copy = send(parts.at[g, s], parts.at[g, s], p_ss.at[i, s], p_rs.at[i, s], at(dx, 0, dc, 0))
+    for half in range(2):
+        for t in queries[half * len(ROW_PEERS) : (half + 1) * len(ROW_PEERS)]:
+            t.wait_recv()
+        for n in range(2):
+            s = 2 * half + n
+            code = tab_s[g, s, 0, 0]
+            owner, blk = code // 4, code % 4
+            src = (owner // 64) * NC + (owner // 2) % NC
+            r = owner % 2
+            q = got[half][src, 4 * n : 4 * n + 4].reshape(ROWS, WIDTH)
+            lens = got[half][src, 8].astype(F32)
+            hi = jnp.where(r == 0, lens[4 * n : 4 * n + 1], lens[4 * n + 2 : 4 * n + 3])
+            lo = jnp.where(r == 0, lens[4 * n + 1 : 4 * n + 2], lens[4 * n + 3 : 4 * n + 4])
+            left = (hi * 64.0 + lo)[:, :1] - (blk * BLOCK).astype(F32)
+            scores = lax.dot_general(
+                q, kv[s, :, :WIDTH], (((1,), (1,)), ((), ())), preferred_element_type=F32
+            ) * SCALE
+            scores = jnp.where(lane_pos < left, scores, -jnp.inf)
+            top = jnp.max(scores, axis=1, keepdims=True)
+            weights = jnp.exp(scores - top)
+            total = jnp.sum(weights, axis=1, keepdims=True)
+            part = jnp.dot(weights.astype(BF16), kv[s, :, WIDTH:], preferred_element_type=F32) / total
+            parts[g, s] = part.astype(BF16).reshape(4, 16, WIDTH)
+            lcols = jnp.where(lane_id == s, top + jnp.log(total), lcols)
+        mine = parts.at[g, 2 * half : 2 * half + 2]
+        for i, (dx, dc) in enumerate(GATHER):
+            copy = send(mine, mine, p_ss.at[i, half], p_rs.at[i, half], at(dx, 0, dc, 0))
             copy.start()
             back.append(copy)
     lt = jnp.concatenate([lcols, lcols], axis=0).T
     for s in range(SLOTS):
         lses[g, s] = lt[s : s + 1]
-    for i, (dx, dc) in enumerate(ROW_PEERS):
+    lse_sent = []
+    for i, (dx, dc) in enumerate(GATHER):
         copy = send(lses.at[g], lses.at[g], l_ss.at[i], l_rs.at[i], at(dx, 0, dc, 0))
         copy.start()
-        back.append(copy)
-    for copy in back:
+        lse_sent.append(copy)
+    handed = []
+    for half in range(2):
+        for i, (dx, _) in enumerate(GATHER[:3]):
+            back[half * len(GATHER) + i].wait_recv()
+            there = parts.at[((x - dx + NX) % NX) * NC + c, 2 * half : 2 * half + 2]
+            copy = send(there, there, u_ss.at[i, half], u_rs.at[i, half], at(0, 0, 1, 0))
+            copy.start()
+            handed.append(copy)
+    for i, (dx, _) in enumerate(GATHER[:3]):
+        lse_sent[i].wait_recv()
+        there = lses.at[((x - dx + NX) % NX) * NC + c]
+        copy = send(there, there, v_ss.at[i], v_rs.at[i], at(0, 0, 1, 0))
+        copy.start()
+        handed.append(copy)
+    for half in range(2):
+        back[half * len(GATHER) + 3].wait_recv()
+    lse_sent[3].wait_recv()
+    for copy in handed:
         copy.wait_recv()
+    back = back + lse_sent + handed
 
     half = lax.broadcasted_iota(jnp.int32, (1, WIDTH), 1) < ROWS
     wmat[...] = jnp.zeros((WIDTH, WIDTH), F32)
@@ -318,24 +355,30 @@
 
 def shards(query, fresh_key_value, kv_pool, lengths, slot_owner, slot_block):
     steps, req_dev, width = query.shape
-    q = jnp.transpose(query.reshape(steps, req_dev, 16, WIDTH), (1, 0, 2, 3)).reshape(8, 16, WIDTH)
     dma = pltpu.SemaphoreType.DMA
-    vmem, smem = pl.BlockSpec(memory_space=pltpu.VMEM), pl.BlockSpec(memory_space=pltpu.SMEM)
+    hbm = pl.BlockSpec(memory_space=pl.ANY)
     n, m = len(ROW_PEERS), len(FORWARD)
     out = pl.pallas_call(
         kernel,
         out_shape=jax.ShapeDtypeStruct((8, 16, WIDTH), BF16),
-        in_specs=[vmem, vmem, pl.BlockSpec(memory_space=pl.ANY), smem, smem, smem],
-        out_specs=vmem,
+        in_specs=[hbm] * 6,
+        out_specs=pl.BlockSpec(memory_space=pltpu.VMEM),
         scratch_shapes=[
+            pltpu.VMEM(query.shape, BF16),
+            pltpu.VMEM((8, 16, WIDTH), BF16),
+            pltpu.VMEM(fresh_key_value.shape, BF16),
+            pltpu.SMEM(lengths.shape, jnp.int32),
+            pltpu.SMEM(slot_owner.shape, jnp.int32),
+            pltpu.SMEM(slot_block.shape, jnp.int32),
             pltpu.VMEM((SLOTS, BLOCK, 2 * WIDTH), BF16),
             pltpu.VMEM((NZ, 9, 16, WIDTH), BF16),
             pltpu.VMEM((GROUPS, SLOTS, 1, WIDTH), jnp.int32),
             pltpu.VMEM((2, 1, WIDTH), jnp.int32),
             pltpu.SMEM((GROUPS, SLOTS, 1, WIDTH), jnp.int32),
             pltpu.SMEM((2, 1, WIDTH), jnp.int32),
-            pltpu.VMEM((n, 17, 16, WIDTH), BF16),
-            pltpu.VMEM((GROUPS, 17, 16, WIDTH), BF16),
+            pltpu.VMEM((n, 2, 9, 16, WIDTH), BF16),
+            pltpu.VMEM((GROUPS, 9, 16, WIDTH), BF16),
+            pltpu.VMEM((GROUPS, 9, 16, WIDTH), BF16),
             pltpu.VMEM((GROUPS, SLOTS, 4, 16, WIDTH), BF16),
             pltpu.VMEM((GROUPS, SLOTS, 1, WIDTH), F32),
             pltpu.VMEM((3, NZ, WIDTH), F32),
@@ -351,25 +394,28 @@
             pltpu.VMEM((4, 1, WIDTH), F32),
             pltpu.VMEM((2, ROWS, WIDTH), F32),
             pltpu.VMEM((2, ROWS, WIDTH), F32),
+            dma((5,)),
             dma((SLOTS,)),
             dma((3,)), dma((3,)),
             dma((n,)), dma((n,)),
             dma((2,)),
             dma((4,)), dma((4,)),
             dma((m,)), dma((m,)),
-            dma((n,)), dma((n,)),
-            dma((n, SLOTS)), dma((n, SLOTS)),
-            dma((n,)), dma((n,)),
+            dma((n, 2)), dma((n, 2)),
+            dma((4, 2)), dma((4, 2)),
+            dma((4,)), dma((4,)),
+            dma((3, 2)), dma((3, 2)),
+            dma((3,)), dma((3,)),
             dma((m,)), dma((m,)),
             dma((m,)), dma((m,)),
             dma((4,)), dma((4,)),
             dma((4,)), dma((4,)),
         ],
         compiler_params=pltpu.CompilerParams(
-            collective_id=0, has_side_effects=True, vmem_limit_bytes=40 << 20
+            collective_id=0, has_side_effects=True, vmem_limit_bytes=60 << 20
         ),
         name="lent_attention",
-    )(q, fresh_key_value, kv_pool, lengths, slot_owner, slot_block)
+    )(query, fresh_key_value, kv_pool, lengths, slot_owner, slot_block)
     out = jnp.transpose(out.reshape(req_dev, steps, 16, WIDTH), (1, 0, 2, 3))
     return out.reshape(steps, req_dev, width)
 

time: 74.5 us -> 66.5 us (0.89)
  the two profiles are of different devices: /device:TPU:8 before, /device:TPU:24 now
where the time goes in v2:
time: 66.5 us; the launch traced here: 66 us
  Pallas kernels  63.3 us (95%)
  local copies, waits for them, and re-layouts  1.42 us (2%)
  between operations  1.31 us (2%)
    pallas_call x1, Pallas kernels, shards(): pl.pallas_call(kernel, out_shape=jax.ShapeDtypeStruct((8, 16, WIDTH), BF1...  63.3 us
    reshape x2, local copies, waits for them, and re-layouts, shards(): return out.reshape(steps, req_dev, width)  1.42 us

profile of v2, /device:TPU:24, one launch (start us, length us, event | category | flops | bytes accessed | tf_op | source)
XLA Modules:
  0.0 66.0 jit_solution(2859817917472802940)
XLA Ops:
  1.3 63.3 %lent_attention.1 = bf16[8,16,128]{2,1,0:T(8,128)(2,1)} custom-call(bf16[4,2,2048]{2,1,0:T(2,128)(2,1)} %q_in.1, bf16[4,2,256]{2,1,0:T(2,128)(2,1)} %fresh_in.1, bf16[4,2048,256]{2,1,0:T(8,128)(2,1)} %kv_ref.1, s32[2]{0:T(128)} %len_in.1, s32[1]{0:T(128)S(6)} %copy.9.owner_in, s32[1]{0:T(128)S(6)} %copy.10.block_in), custom_call_target="tpu_custom_call" | custom-call | tf_op jit(solution)/shard_map/lent_attention/pallas_call | solution.py:361
  64.6 0.8 %reshape.8 = bf16[4,2,2048]{2,0,1:T(4,128)(2,1)S(1)} reshape(bf16[4,2,16,128]{3,2,0,1:T(8,128)(2,1)} %bitcast.7) | data formatting | bytes 65536 | tf_op jit(solution)/shard_map/reshape | solution.py:420
  65.4 0.7 copy.8

commit v3 on v2

v3 whole, which is shorter than its diff:
```python
import math

import jax
import jax.numpy as jnp
from jax import lax
from jax.experimental import pallas as pl
from jax.experimental.pallas import tpu as pltpu
from jax.sharding import PartitionSpec as P

BLOCK = 2048
WIDTH = 128
ROWS = 64
NX, NZ, NC, NY = 4, 16, 2, 4
GROUPS = NX * NC
SLOTS = 4
SCALE = 1.0 / math.sqrt(WIDTH)
LOG2E = math.log2(math.e)
NEG = -1e30
F32 = jnp.float32
BF16 = jnp.bfloat16

PARENT = {3: 0, -3: 0, 1: 0, -1: 0, 6: 3, 2: 3, 4: 3, -6: -3, -2: -3, -4: -3, 8: 6, 7: 6, 5: 6, -7: -6, -5: -6}
CHILDREN = {p: [o for o in PARENT if PARENT[o] == p] for p in (0, *PARENT)}
PLACE = {o: i for i, o in enumerate(PARENT)}
NEAR = (3, -3, 2, -2, 1, -1)
X_PEERS = (1, 3, 2)


def kernel(
    q_in, fresh_in, kv_ref, len_in, owner_in, block_in, out_ref,
    q_raw, q_ref, fresh_ref, len_ref, owner_ref, block_ref,
    kv, kt, qall, rowtab, ivec, tab_s, ivec_s, sel, got0, got1, parts, lses, lrow, wmat, wcol,
    cbuf, clse, rbuf, rlse, mbuf, mlse, tail, tail_lse,
    in_sem, kv_sem, sm_sem, y_ss, y_rs, t_ss, t_rs, w_ss, w_rs, a_ss, a_rs, h_ss, h_rs, s_ss, s_rs,
    p_ss, p_rs, l_ss, l_rs, u_ss, u_rs, v_ss, v_rs, c_ss, c_rs, d_ss, d_rs,
):
    me = lax.axis_index("inst")
    y = lax.axis_index("tp")
    x, z, c = me // (NZ * NC), (me // NC) % NZ, me % NC
    g = x * NC + c

    def at(dx, dz, dc, dy):
        xx, zz = (x + dx + NX) % NX, (z + dz + NZ) % NZ
        cc, yy = (c + dc) % NC, (y + dy) % NY
        return ((xx * NZ + zz) * NC + cc, yy)

    def send(src, dst, ss, rs, to):
        return pltpu.make_async_remote_copy(
            src_ref=src, dst_ref=dst, send_sem=ss, recv_sem=rs,
            device_id=to, device_id_type=pl.DeviceIdType.MESH,
        )

    peers = [at(0, d, 0, 0) for d in NEAR]
    peers += [at(dx, 0, 0, 0) for dx in X_PEERS] + [at(0, 0, 1, 0)]
    peers += [at(0, 0, 0, d) for d in range(1, NY)]
    barrier = pltpu.get_barrier_semaphore()
    for p in peers:
        pl.semaphore_signal(barrier, inc=1, device_id=p, device_id_type=pl.DeviceIdType.MESH)
    inputs = [
        pltpu.make_async_copy(a, b, in_sem.at[i])
        for i, (a, b) in enumerate(
            ((q_in, q_raw), (len_in, len_ref), (owner_in, owner_ref), (block_in, block_ref), (fresh_in, fresh_ref))
        )
    ]
    for copy in inputs:
        copy.start()
    kv_copies = [pltpu.make_async_copy(kv_ref.at[s], kv.at[s], kv_sem.at[s]) for s in range(SLOTS)]
    for copy in kv_copies:
        copy.start()
    for copy in inputs:
        copy.wait()
    for a in range(4):
        qa = q_raw[a].astype(F32)
        for r in range(2):
            tile = jnp.concatenate([qa[r : r + 1, WIDTH * h : WIDTH * (h + 1)] for h in range(16)], axis=0)
            q_ref[4 * r + a] = tile.astype(BF16)
    row = lax.broadcasted_iota(jnp.int32, (16, WIDTH), 0) % 4
    hi = jnp.where(row < 2, len_ref[0] // 64, len_ref[1] // 64)
    lo = jnp.where(row < 2, len_ref[0] % 64, len_ref[1] % 64)
    qall[z, c, 0:8] = q_ref[...]
    qall[z, c, 8] = jnp.where(row % 2 == 0, hi, lo).astype(F32).astype(BF16)
    rowtab[g, y] = jnp.full((1, WIDTH), owner_ref[0] * 4 + block_ref[0], jnp.int32)
    pl.semaphore_wait(barrier, len(peers))

    sent = []
    spread, hand = {}, []

    def pass_on(o):
        came = qall.at[(z - o + NZ) % NZ, c]
        for k in CHILDREN[o]:
            i = PLACE[k]
            spread[k] = send(came, came, a_ss.at[i], a_rs.at[i], at(0, k - o, 0, 0))
            spread[k].start()
        i = PLACE.get(o, len(PLACE))
        hand.append(send(came, came, h_ss.at[i], h_rs.at[i], at(0, 0, 1, 0)))
        hand[-1].start()

    def arrive(*places):
        for o in places:
            spread[o].wait_recv()
            pass_on(o)

    pass_on(0)
    tables = []
    for i in range(NY - 1):
        tables.append(send(rowtab.at[g, y], rowtab.at[g, y], y_ss.at[i], y_rs.at[i], at(0, 0, 0, i + 1)))
        tables[-1].start()
    for t in tables:
        t.wait_recv()
    along_x, across = [], []
    for i, dx in enumerate(X_PEERS):
        along_x.append(send(rowtab.at[g], rowtab.at[g], t_ss.at[i], t_rs.at[i], at(dx, 0, 0, 0)))
        along_x[-1].start()

    def table_to_sibling(i, gg):
        across.append(send(rowtab.at[gg], rowtab.at[gg], w_ss.at[i], w_rs.at[i], at(0, 0, 1, 0)))
        across[-1].start()

    table_to_sibling(3, g)

    for r in range(2):
        qf = q_ref[4 * r : 4 * r + 4].reshape(ROWS, WIDTH).astype(F32)
        step = lax.broadcasted_iota(jnp.int32, (ROWS, 1), 0) // 16
        ss = []
        for b in range(4):
            k_b = fresh_ref[b].astype(F32)[r : r + 1, :WIDTH]
            s_b = jnp.sum(qf * k_b, axis=1, keepdims=True) * SCALE
            ss.append(jnp.where(step >= b, s_b, -jnp.inf))
        top = jnp.maximum(jnp.maximum(ss[0], ss[1]), jnp.maximum(ss[2], ss[3]))
        ws = [jnp.exp(s_b - top) for s_b in ss]
        total = ws[0] + ws[1] + ws[2] + ws[3]
        acc = jnp.zeros((ROWS, WIDTH), F32)
        for b in range(4):
            v_b = fresh_ref[b].astype(F32)[r : r + 1, WIDTH:]
            acc = acc + ws[b].astype(BF16).astype(F32) * v_b
        tail[r] = acc / total
        tail_lse[r] = jnp.broadcast_to(top + jnp.log(total), (ROWS, WIDTH))

    arrive(1, -1, 3, -3)

    for s in range(SLOTS):
        kv_copies[s].wait()
        kt[s] = kv[s, :, :WIDTH].T

    for i, dx in enumerate(X_PEERS):
        along_x[i].wait_recv()
        table_to_sibling(i, ((x - dx + NX) % NX) * NC + c)
    arrive(2, 4, -2, -4, 6, -6)

    for t in across:
        t.wait_recv()
    lane = lax.broadcasted_iota(jnp.int32, (1, WIDTH), 1)
    want = (((x * NZ + (lane % 32) // 2) * NC + c) * 2 + lane % 2) * 4 + lane // 32
    index = jnp.zeros((1, WIDTH), jnp.int32)
    count = jnp.zeros((1, WIDTH), jnp.int32)
    for gg in range(GROUPS):
        for s in range(SLOTS):
            hit = rowtab[gg, s] == want
            index = jnp.where(hit, gg * SLOTS + s, index)
            count = jnp.where(hit, 1, count)
    ivec[0] = index
    ivec[1] = count
    to_smem = [
        pltpu.make_async_copy(rowtab, tab_s, sm_sem.at[0]),
        pltpu.make_async_copy(ivec, ivec_s, sm_sem.at[1]),
    ]
    for copy in to_smem:
        copy.start()
    for copy in to_smem:
        copy.wait()

    arrive(5, 7, -5, -7, 8)
    for t in hand:
        t.wait_recv()

    group = lax.broadcasted_iota(jnp.int32, (16, WIDTH), 0) // 4
    got = (got0, got1)

    def choose(gg, half, ref):
        lens = jnp.zeros((16, WIDTH), F32)
        for i in range(2):
            owner = tab_s[gg, 2 * half + i, 0, 0] // 4
            zz, cc, r = (owner // 4) % NZ, (owner // 2) % NC, owner % 2
            ref[4 * i : 4 * i + 4] = qall[zz, cc, pl.ds(4 * r, 4)]
            lens = jnp.where(group == i, qall[zz, cc, 8].astype(F32), lens)
        ref[8] = lens.astype(BF16)

    queries = []
    for half in range(2):
        for i, dx in enumerate(X_PEERS):
            choose(((x + dx) % NX) * NC + c, half, sel.at[i, half])
            copy = send(
                sel.at[i, half], got[half].at[x], s_ss.at[i, half], s_rs.at[i, half], at(dx, 0, 0, 0)
            )
            copy.start()
            queries.append(copy)
        choose(g, half, got[half].at[x])

    lane_pos = lax.broadcasted_iota(jnp.int32, (1, BLOCK), 1).astype(F32)
    lane_id = lax.broadcasted_iota(jnp.int32, (ROWS, WIDTH), 1)
    lcols = jnp.zeros((ROWS, WIDTH), F32)
    back = []
    for half in range(2):
        for t in queries[half * len(X_PEERS) : (half + 1) * len(X_PEERS)]:
            t.wait_recv()
        for n in range(2):
            s = 2 * half + n
            code = tab_s[g, s, 0, 0]
            owner, blk = code // 4, code % 4
            src = owner // 64
            r = owner % 2
            q = got[half][src, 4 * n : 4 * n + 4].reshape(ROWS, WIDTH)
            lens = got[half][src, 8].astype(F32)
            hi = jnp.where(r == 0, lens[4 * n : 4 * n + 1], lens[4 * n + 2 : 4 * n + 3])
            lo = jnp.where(r == 0, lens[4 * n + 1 : 4 * n + 2], lens[4 * n + 3 : 4 * n + 4])
            left = (hi * 64.0 + lo)[:, :1] - (blk * BLOCK).astype(F32)
            scores = jnp.dot(q, kt[s], preferred_element_type=F32)
            scores = jnp.where(lane_pos < left, scores, -jnp.inf)
            top = jnp.max(scores, axis=1, keepdims=True)
            weights = jnp.exp2((scores - top) * (SCALE * LOG2E))
            total = jnp.sum(weights, axis=1, keepdims=True)
            part = jnp.dot(weights.astype(BF16), kv[s, :, WIDTH:], preferred_element_type=F32) / total
            parts[g, s] = part.astype(BF16).reshape(4, 16, WIDTH)
            lcols = jnp.where(lane_id == s, top * SCALE + jnp.log(total), lcols)
        mine = parts.at[g, 2 * half : 2 * half + 2]
        for i in range(4):
            to = at(X_PEERS[i], 0, 0, 0) if i < 3 else at(0, 0, 1, 0)
            copy = send(mine, mine, p_ss.at[i, half], p_rs.at[i, half], to)
            copy.start()
            back.append(copy)
    lt = jnp.concatenate([lcols, lcols], axis=0).T
    for s in range(SLOTS):
        lses[g, s] = lt[s : s + 1]
    lse_sent = []
    for i in range(4):
        to = at(X_PEERS[i], 0, 0, 0) if i < 3 else at(0, 0, 1, 0)
        copy = send(lses.at[g], lses.at[g], l_ss.at[i], l_rs.at[i], to)
        copy.start()
        lse_sent.append(copy)
    handed = []
    for half in range(2):
        for i, dx in enumerate(X_PEERS):
            back[half * 4 + i].wait_recv()
            there = parts.at[((x - dx + NX) % NX) * NC + c, 2 * half : 2 * half + 2]
            copy = send(there, there, u_ss.at[i, half], u_rs.at[i, half], at(0, 0, 1, 0))
            copy.start()
            handed.append(copy)
    for i, dx in enumerate(X_PEERS):
        lse_sent[i].wait_recv()
        there = lses.at[((x - dx + NX) % NX) * NC + c]
        copy = send(there, there, v_ss.at[i], v_rs.at[i], at(0, 0, 1, 0))
        copy.start()
        handed.append(copy)
    for half in range(2):
        back[half * 4 + 3].wait_recv()
    lse_sent[3].wait_recv()
    for copy in handed:
        copy.wait_recv()
    back = back + lse_sent + handed

    half = lax.broadcasted_iota(jnp.int32, (1, WIDTH), 1) < ROWS
    wmat[...] = jnp.zeros((WIDTH, WIDTH), F32)

    def where_is(d, r, k):
        j = k * 32 + ((z + d) % NZ) * 2 + r
        return ivec_s[0, 0, j], ivec_s[1, 0, j]

    for d in range(NZ):
        for k in range(3):
            pair = []
            for r in range(2):
                i, n = where_is(d, r, k)
                pair.append(jnp.where(n > 0, lses[i // 4, i % 4], NEG))
            lrow[k, d] = jnp.where(half, pair[0], pair[1])[0]
    l0, l1, l2 = lrow[0], lrow[1], lrow[2]
    peak = jnp.maximum(jnp.maximum(l0, l1), l2)
    w0, w1, w2 = jnp.exp(l0 - peak), jnp.exp(l1 - peak), jnp.exp(l2 - peak)
    total = w0 + w1 + w2
    merged = peak + jnp.log(total)
    wmat[0:16] = w0 / total
    wmat[16:32] = w1 / total
    wmat[32:48] = w2 / total
    for d in range(NZ):
        clse[d] = merged[d : d + 1]
    wcol[...] = wmat[...].T

    def build(d):
        d = d % NZ
        for r in range(2):
            acc = jnp.zeros((ROWS, WIDTH), F32)
            for k in range(3):
                i, _ = where_is(d, r, k)
                p = parts[i // 4, i % 4].reshape(ROWS, WIDTH).astype(F32)
                acc = acc + wcol[r * ROWS : (r + 1) * ROWS, k * 16 + d : k * 16 + d + 1] * p
            cbuf[d, 4 * r : 4 * r + 4] = acc.astype(BF16).reshape(4, 16, WIDTH)

    up = {}

    def send_up(o, data, lse):
        i = PLACE[o]
        to = at(0, PARENT[o] - o, 0, 0)
        up[o] = (
            send(data, rbuf.at[i], c_ss.at[i], c_rs.at[i], to),
            send(lse, rlse.at[i], d_ss.at[i], d_rs.at[i], to),
        )
        for copy in up[o]:
            copy.start()

    def gather_up(o):
        for k in CHILDREN[o]:
            for copy in up[k]:
                copy.wait_recv()

    for o in (5, 7, 8, -5, -7, 2, 4, -2, -4, 1, -1):
        build(-o)
        send_up(o, cbuf.at[-o % NZ], clse.at[-o % NZ])
    for o in (6, -6, 3, -3, 0):
        build(-o)
    for n, o in enumerate((6, -6, 3, -3)):
        gather_up(o)
        ls = [clse[-o % NZ]] + [rlse[PLACE[k]] for k in CHILDREN[o]]
        data = [cbuf[-o % NZ]] + [rbuf[PLACE[k]] for k in CHILDREN[o]]
        peak = ls[0]
        for l in ls[1:]:
            peak = jnp.maximum(peak, l)
        ws = [jnp.exp(l - peak) for l in ls]
        total = ws[0]
        for w in ws[1:]:
            total = total + w
        mlse[n] = peak + jnp.log(total)
        for i, w in enumerate(ws):
            wmat[i : i + 1] = w / total
        wt = wmat[...].T
        acc = jnp.zeros((WIDTH, WIDTH), F32)
        for i, p in enumerate(data):
            acc = acc + wt[:, i : i + 1] * p.reshape(WIDTH, WIDTH).astype(F32)
        mbuf[n] = acc.astype(BF16).reshape(8, 16, WIDTH)
        send_up(o, mbuf.at[n], mlse.at[n])
    gather_up(0)
    for i, k in enumerate(CHILDREN[0]):
        wmat[i : i + 1] = rlse[PLACE[k]]
    wmat[4:5] = clse[0]
    wt = wmat[...].T
    done = []
    for r in range(2):
        rs = slice(r * ROWS, (r + 1) * ROWS)
        tl = tail_lse[r][:, :1]
        ls = [wt[rs, n : n + 1] for n in range(5)]
        peak = tl
        for l in ls:
            peak = jnp.maximum(peak, l)
        w = jnp.exp(tl - peak)
        denom = w
        acc = w * tail[r]
        for n, ref in enumerate([rbuf.at[PLACE[k]] for k in CHILDREN[0]] + [cbuf.at[0]]):
            w = jnp.exp(ls[n] - peak)
            denom = denom + w
            acc = acc + w * ref[4 * r : 4 * r + 4].reshape(ROWS, WIDTH).astype(F32)
        done.append(acc / denom)
    for a in range(4):
        heads = [
            jnp.concatenate([done[0][i : i + 1], done[1][i : i + 1]], axis=0)
            for i in range(16 * a, 16 * a + 16)
        ]
        out_ref[a] = jnp.concatenate(heads, axis=1).astype(BF16)

    for copy in [*spread.values(), *hand, *tables, *along_x, *across, *queries, *back]:
        copy.wait_send()
    for pair in up.values():
        for copy in pair:
            copy.wait_send()


def shards(query, fresh_key_value, kv_pool, lengths, slot_owner, slot_block):
    dma = pltpu.SemaphoreType.DMA
    hbm = pl.BlockSpec(memory_space=pl.ANY)
    m = len(PARENT)
    return pl.pallas_call(
        kernel,
        out_shape=jax.ShapeDtypeStruct(query.shape, BF16),
        in_specs=[hbm] * 6,
        out_specs=pl.BlockSpec(memory_space=pltpu.VMEM),
        scratch_shapes=[
            pltpu.VMEM(query.shape, BF16),
            pltpu.VMEM((8, 16, WIDTH), BF16),
            pltpu.VMEM(fresh_key_value.shape, BF16),
            pltpu.SMEM(lengths.shape, jnp.int32),
            pltpu.SMEM(slot_owner.shape, jnp.int32),
            pltpu.SMEM(slot_block.shape, jnp.int32),
            pltpu.VMEM((SLOTS, BLOCK, 2 * WIDTH), BF16),
            pltpu.VMEM((SLOTS, WIDTH, BLOCK), BF16),
            pltpu.VMEM((NZ, NC, 9, 16, WIDTH), BF16),
            pltpu.VMEM((GROUPS, SLOTS, 1, WIDTH), jnp.int32),
            pltpu.VMEM((2, 1, WIDTH), jnp.int32),
            pltpu.SMEM((GROUPS, SLOTS, 1, WIDTH), jnp.int32),
            pltpu.SMEM((2, 1, WIDTH), jnp.int32),
            pltpu.VMEM((3, 2, 9, 16, WIDTH), BF16),
            pltpu.VMEM((NX, 9, 16, WIDTH), BF16),
            pltpu.VMEM((NX, 9, 16, WIDTH), BF16),
            pltpu.VMEM((GROUPS, SLOTS, 4, 16, WIDTH), BF16),
            pltpu.VMEM((GROUPS, SLOTS, 1, WIDTH), F32),
            pltpu.VMEM((3, NZ, WIDTH), F32),
            pltpu.VMEM((WIDTH, WIDTH), F32),
            pltpu.VMEM((WIDTH, WIDTH), F32),
            pltpu.VMEM((NZ, 8, 16, WIDTH), BF16),
            pltpu.VMEM((NZ, 1, WIDTH), F32),
            pltpu.VMEM((m, 8, 16, WIDTH), BF16),
            pltpu.VMEM((m, 1, WIDTH), F32),
            pltpu.VMEM((4, 8, 16, WIDTH), BF16),
            pltpu.VMEM((4, 1, WIDTH), F32),
            pltpu.VMEM((2, ROWS, WIDTH), F32),
            pltpu.VMEM((2, ROWS, WIDTH), F32),
            dma((5,)),
            dma((SLOTS,)),
            dma((2,)),
            dma((3,)), dma((3,)),
            dma((3,)), dma((3,)),
            dma((4,)), dma((4,)),
            dma((m,)), dma((m,)),
            dma((m + 1,)), dma((m + 1,)),
            dma((3, 2)), dma((3, 2)),
            dma((4, 2)), dma((4, 2)),
            dma((4,)), dma((4,)),
            dma((3, 2)), dma((3, 2)),
            dma((3,)), dma((3,)),
            dma((m,)), dma((m,)),
            dma((m,)), dma((m,)),
        ],
        compiler_params=pltpu.CompilerParams(
            collective_id=0, has_side_effects=True, vmem_limit_bytes=60 << 20
        ),
        name="lent_attention",
    )(query, fresh_key_value, kv_pool, lengths, slot_owner, slot_block)


def solution(mesh):
    placed = (
        P(None, "inst", "tp"),
        P(None, "inst", "tp"),
        P("inst", None, "tp"),
        P("inst"),
        P(("inst", "tp")),
        P(("inst", "tp")),
    )
    return jax.shard_map(
        shards, mesh=mesh, in_specs=placed, out_specs=P(None, "inst", "tp"), check_vma=False
    )
```

time: 66.5 us -> 64.1 us (0.964)
  Pallas kernels: 63.3 us -> 61.1 us
    pallas_call x1, Pallas kernels: 63.3 us -> 61.1 us  [shards(): pl.pallas_call(kernel, out_shape=jax.ShapeDtypeStruct(query.shape, BF16),...]
    reshape x2 -> x0, local copies, waits for them, and re-layouts: 1.42 us -> none  [shards(): return out.reshape(steps, req_dev, width)]
    unnamed x0 -> x1, local copies, waits for them, and re-layouts: none -> 1.4 us
where the time goes in v3:
time: 64.1 us; the launch traced here: 63.8 us
  Pallas kernels  61.1 us (95%)
  local copies, waits for them, and re-layouts  1.4 us (2%)
  between operations  1.3 us (2%)
    pallas_call x1, Pallas kernels, shards(): pl.pallas_call(kernel, out_shape=jax.ShapeDtypeStruct(query.shape, BF16),...  61.1 us
    unnamed x1, local copies, waits for them, and re-layouts  1.4 us

profile of v3, /device:TPU:24, one launch (start us, length us, event | category | flops | bytes accessed | tf_op | source)
XLA Modules:
  0.0 63.8 jit_solution(3890903888964092554)
XLA Ops:
  1.3 61.1 %lent_attention.1 = bf16[4,2,2048]{2,1,0:T(2,128)(2,1)} custom-call(bf16[4,2,2048]{2,1,0:T(2,128)(2,1)} %q_in.1, bf16[4,2,256]{2,1,0:T(2,128)(2,1)} %fresh_in.1, bf16[4,2048,256]{2,1,0:T(8,128)(2,1)} %kv_ref.1, s32[2]{0:T(128)} %len_in.1, s32[1]{0:T(128)S(6)} %copy.8.owner_in, s32[1]{0:T(128)S(6)} %copy.9.block_in), custom_call_target="tpu_custom_call" | custom-call | tf_op jit(solution)/shard_map/lent_attention/pallas_call | solution.py:378
  62.4 1.4 %copy.10 = bf16[4,2,2048]{2,1,0:T(2,128)(2,1)} copy(bf16[4,2,2048]{2,1,0:T(2,128)(2,1)} %lent_attention.1) | data formatting | bytes 65536

commit v4 on v3

--- a/solution.py
+++ b/solution.py
@@ -23,7 +23,7 @@
 CHILDREN = {p: [o for o in PARENT if PARENT[o] == p] for p in (0, *PARENT)}
 PLACE = {o: i for i, o in enumerate(PARENT)}
 NEAR = (3, -3, 2, -2, 1, -1)
-X_PEERS = (1, 3, 2)
+X_PEERS = (2, 1, 3)
 
 
 def kernel(
@@ -199,10 +199,11 @@
     lane_pos = lax.broadcasted_iota(jnp.int32, (1, BLOCK), 1).astype(F32)
     lane_id = lax.broadcasted_iota(jnp.int32, (ROWS, WIDTH), 1)
     lcols = jnp.zeros((ROWS, WIDTH), F32)
-    back = []
+    back, lse_sent = [], []
     for half in range(2):
         for t in queries[half * len(X_PEERS) : (half + 1) * len(X_PEERS)]:
             t.wait_recv()
+        rounded, totals = [], []
         for n in range(2):
             s = 2 * half + n
             code = tab_s[g, s, 0, 0]
@@ -219,44 +220,53 @@
             top = jnp.max(scores, axis=1, keepdims=True)
             weights = jnp.exp2((scores - top) * (SCALE * LOG2E))
             total = jnp.sum(weights, axis=1, keepdims=True)
-            part = jnp.dot(weights.astype(BF16), kv[s, :, WIDTH:], preferred_element_type=F32) / total
+            lcols = jnp.where(lane_id == s, top * SCALE + jnp.log(total), lcols)
+            rounded.append(weights.astype(BF16))
+            totals.append(total)
+        if half == 1:
+            lt = jnp.concatenate([lcols, lcols], axis=0).T
+            for s in range(SLOTS):
+                lses[g, s] = lt[s : s + 1]
+            for i in range(4):
+                to = at(X_PEERS[i], 0, 0, 0) if i < 3 else at(0, 0, 1, 0)
+                copy = send(lses.at[g], lses.at[g], l_ss.at[i], l_rs.at[i], to)
+                copy.start()
+                lse_sent.append(copy)
+        for n in range(2):
+            s = 2 * half + n
+            part = jnp.dot(rounded[n], kv[s, :, WIDTH:], preferred_element_type=F32) / totals[n]
             parts[g, s] = part.astype(BF16).reshape(4, 16, WIDTH)
-            lcols = jnp.where(lane_id == s, top * SCALE + jnp.log(total), lcols)
         mine = parts.at[g, 2 * half : 2 * half + 2]
         for i in range(4):
             to = at(X_PEERS[i], 0, 0, 0) if i < 3 else at(0, 0, 1, 0)
             copy = send(mine, mine, p_ss.at[i, half], p_rs.at[i, half], to)
             copy.start()
             back.append(copy)
-    lt = jnp.concatenate([lcols, lcols], axis=0).T
-    for s in range(SLOTS):
-        lses[g, s] = lt[s : s + 1]
-    lse_sent = []
-    for i in range(4):
-        to = at(X_PEERS[i], 0, 0, 0) if i < 3 else at(0, 0, 1, 0)
-        copy = send(lses.at[g], lses.at[g], l_ss.at[i], l_rs.at[i], to)
-        copy.start()
-        lse_sent.append(copy)
+    for copy in [*spread.values(), *hand, *tables, *along_x, *across, *queries]:
+        copy.wait_send()
+
     handed = []
-    for half in range(2):
+
+    def hand_parts(half):
         for i, dx in enumerate(X_PEERS):
             back[half * 4 + i].wait_recv()
             there = parts.at[((x - dx + NX) % NX) * NC + c, 2 * half : 2 * half + 2]
             copy = send(there, there, u_ss.at[i, half], u_rs.at[i, half], at(0, 0, 1, 0))
             copy.start()
             handed.append(copy)
+
+    hand_parts(0)
+    lse_handed = []
     for i, dx in enumerate(X_PEERS):
         lse_sent[i].wait_recv()
         there = lses.at[((x - dx + NX) % NX) * NC + c]
         copy = send(there, there, v_ss.at[i], v_rs.at[i], at(0, 0, 1, 0))
         copy.start()
-        handed.append(copy)
-    for half in range(2):
-        back[half * 4 + 3].wait_recv()
+        lse_handed.append(copy)
+    hand_parts(1)
     lse_sent[3].wait_recv()
-    for copy in handed:
+    for copy in lse_handed:
         copy.wait_recv()
-    back = back + lse_sent + handed
 
     half = lax.broadcasted_iota(jnp.int32, (1, WIDTH), 1) < ROWS
     wmat[...] = jnp.zeros((WIDTH, WIDTH), F32)
@@ -294,6 +304,11 @@
                 acc = acc + wcol[r * ROWS : (r + 1) * ROWS, k * 16 + d : k * 16 + d + 1] * p
             cbuf[d, 4 * r : 4 * r + 4] = acc.astype(BF16).reshape(4, 16, WIDTH)
 
+    for half in range(2):
+        back[half * 4 + 3].wait_recv()
+    for copy in handed:
+        copy.wait_recv()
+
     up = {}
 
     def send_up(o, data, lse):
@@ -316,6 +331,8 @@
         send_up(o, cbuf.at[-o % NZ], clse.at[-o % NZ])
     for o in (6, -6, 3, -3, 0):
         build(-o)
+    for copy in [*back, *lse_sent, *handed, *lse_handed]:
+        copy.wait_send()
     for n, o in enumerate((6, -6, 3, -3)):
         gather_up(o)
         ls = [clse[-o % NZ]] + [rlse[PLACE[k]] for k in CHILDREN[o]]
@@ -330,17 +347,21 @@
         mlse[n] = peak + jnp.log(total)
         for i, w in enumerate(ws):
             wmat[i : i + 1] = w / total
-        wt = wmat[...].T
+        wt = wmat[0:8].T
         acc = jnp.zeros((WIDTH, WIDTH), F32)
         for i, p in enumerate(data):
             acc = acc + wt[:, i : i + 1] * p.reshape(WIDTH, WIDTH).astype(F32)
         mbuf[n] = acc.astype(BF16).reshape(8, 16, WIDTH)
         send_up(o, mbuf.at[n], mlse.at[n])
+    for o in up:
+        if o not in (3, -3):
+            for copy in up[o]:
+                copy.wait_send()
     gather_up(0)
     for i, k in enumerate(CHILDREN[0]):
         wmat[i : i + 1] = rlse[PLACE[k]]
     wmat[4:5] = clse[0]
-    wt = wmat[...].T
+    wt = wmat[0:8].T
     done = []
     for r in range(2):
         rs = slice(r * ROWS, (r + 1) * ROWS)
@@ -364,10 +385,8 @@
         ]
         out_ref[a] = jnp.concatenate(heads, axis=1).astype(BF16)
 
-    for copy in [*spread.values(), *hand, *tables, *along_x, *across, *queries, *back]:
-        copy.wait_send()
-    for pair in up.values():
-        for copy in pair:
+    for o in (3, -3):
+        for copy in up[o]:
             copy.wait_send()
 
 

time: 64.1 us -> 62.2 us (0.970)
  Pallas kernels: 61.1 us -> 59.2 us
    pallas_call x1, Pallas kernels: 61.1 us -> 59.2 us  [shards(): pl.pallas_call(kernel, out_shape=jax.ShapeDtypeStruct(query.shape, BF16),...]
where the time goes in v4:
time: 62.2 us; the launch traced here: 61.9 us
  Pallas kernels  59.2 us (95%)
  local copies, waits for them, and re-layouts  1.4 us (2%)
  between operations  1.3 us (2%)
    pallas_call x1, Pallas kernels, shards(): pl.pallas_call(kernel, out_shape=jax.ShapeDtypeStruct(query.shape, BF16),...  59.2 us
    unnamed x1, local copies, waits for them, and re-layouts  1.4 us

profile of v4, /device:TPU:24, one launch (start us, length us, event | category | flops | bytes accessed | tf_op | source)
XLA Modules:
  0.0 61.9 jit_solution(14460284486702870196)
XLA Ops:
  1.3 59.2 %lent_attention.1 = bf16[4,2,2048]{2,1,0:T(2,128)(2,1)} custom-call(bf16[4,2,2048]{2,1,0:T(2,128)(2,1)} %q_in.1, bf16[4,2,256]{2,1,0:T(2,128)(2,1)} %fresh_in.1, bf16[4,2048,256]{2,1,0:T(8,128)(2,1)} %kv_ref.1, s32[2]{0:T(128)} %len_in.1, s32[1]{0:T(128)S(6)} %copy.8.owner_in, s32[1]{0:T(128)S(6)} %copy.9.block_in), custom_call_target="tpu_custom_call" | custom-call | tf_op jit(solution)/shard_map/lent_attention/pallas_call | solution.py:397
  60.5 1.4 %copy.10 = bf16[4,2,2048]{2,1,0:T(2,128)(2,1)} copy(bf16[4,2,2048]{2,1,0:T(2,128)(2,1)} %lent_attention.1) | data formatting | bytes 65536

commit v5 on v4

--- a/solution.py
+++ b/solution.py
@@ -19,17 +19,32 @@
 F32 = jnp.float32
 BF16 = jnp.bfloat16
 
+DOWN = {3: 0, -3: 0, 1: 0, -1: 0, 6: 3, 2: 3, 4: 3, -6: -3, -2: -3, -4: -3, 8: 6, 7: 6, 5: 6, -7: -6, -5: -6}
 PARENT = {3: 0, -3: 0, 1: 0, -1: 0, 6: 3, 2: 3, 4: 3, -6: -3, -2: -3, -4: -3, 8: 6, 7: 6, 5: 6, -7: -6, -5: -6}
+
+
+def level(tree, o):
+    return 0 if o == 0 else 1 + level(tree, tree[o])
+
+
+def height(tree, o):
+    return max([0] + [1 + height(tree, k) for k in tree if tree[k] == o])
+
+
+BELOW = {p: [o for o in DOWN if DOWN[o] == p] for p in (0, *DOWN)}
 CHILDREN = {p: [o for o in PARENT if PARENT[o] == p] for p in (0, *PARENT)}
 PLACE = {o: i for i, o in enumerate(PARENT)}
-NEAR = (3, -3, 2, -2, 1, -1)
+ARRIVE = {n: sorted((o for o in DOWN if level(DOWN, o) == n), key=lambda o: (-height(DOWN, o), abs(o))) for n in range(1, 5)}
+LEAVES = sorted((o for o in PARENT if not CHILDREN[o]), key=lambda o: -level(PARENT, o))
+HUBS = sorted((o for o in PARENT if CHILDREN[o]), key=lambda o: height(PARENT, o))
+NEAR = sorted({t * (o - tree[o]) for tree in (DOWN, PARENT) for o in tree for t in (1, -1)}, key=lambda d: -abs(d))
 X_PEERS = (2, 1, 3)
 
 
 def kernel(
     q_in, fresh_in, kv_ref, len_in, owner_in, block_in, out_ref,
     q_raw, q_ref, fresh_ref, len_ref, owner_ref, block_ref,
-    kv, kt, qall, rowtab, ivec, tab_s, ivec_s, sel, got0, got1, parts, lses, lrow, wmat, wcol,
+    kv, kt, qall, rowtab, ivec, tab_s, ivec_s, sel, got0, got1, parts, lses, wmat, wcol,
     cbuf, clse, rbuf, rlse, mbuf, mlse, tail, tail_lse,
     in_sem, kv_sem, sm_sem, y_ss, y_rs, t_ss, t_rs, w_ss, w_rs, a_ss, a_rs, h_ss, h_rs, s_ss, s_rs,
     p_ss, p_rs, l_ss, l_rs, u_ss, u_rs, v_ss, v_rs, c_ss, c_rs, d_ss, d_rs,
@@ -87,7 +102,7 @@
 
     def pass_on(o):
         came = qall.at[(z - o + NZ) % NZ, c]
-        for k in CHILDREN[o]:
+        for k in BELOW[o]:
             i = PLACE[k]
             spread[k] = send(came, came, a_ss.at[i], a_rs.at[i], at(0, k - o, 0, 0))
             spread[k].start()
@@ -136,30 +151,28 @@
         tail[r] = acc / total
         tail_lse[r] = jnp.broadcast_to(top + jnp.log(total), (ROWS, WIDTH))
 
-    arrive(1, -1, 3, -3)
+    arrive(*ARRIVE[1])
 
     for s in range(SLOTS):
         kv_copies[s].wait()
         kt[s] = kv[s, :, :WIDTH].T
 
+    arrive(*(o for o in ARRIVE[2] if BELOW[o]))
     for i, dx in enumerate(X_PEERS):
         along_x[i].wait_recv()
         table_to_sibling(i, ((x - dx + NX) % NX) * NC + c)
-    arrive(2, 4, -2, -4, 6, -6)
+    arrive(*(o for o in ARRIVE[2] if not BELOW[o]))
+    arrive(*(o for o in ARRIVE[3] if BELOW[o]))
 
     for t in across:
         t.wait_recv()
     lane = lax.broadcasted_iota(jnp.int32, (1, WIDTH), 1)
     want = (((x * NZ + (lane % 32) // 2) * NC + c) * 2 + lane % 2) * 4 + lane // 32
     index = jnp.zeros((1, WIDTH), jnp.int32)
-    count = jnp.zeros((1, WIDTH), jnp.int32)
     for gg in range(GROUPS):
         for s in range(SLOTS):
-            hit = rowtab[gg, s] == want
-            index = jnp.where(hit, gg * SLOTS + s, index)
-            count = jnp.where(hit, 1, count)
-    ivec[0] = index
-    ivec[1] = count
+            index = jnp.where(rowtab[gg, s] == want, gg * SLOTS + s, index)
+    ivec[...] = index
     to_smem = [
         pltpu.make_async_copy(rowtab, tab_s, sm_sem.at[0]),
         pltpu.make_async_copy(ivec, ivec_s, sm_sem.at[1]),
@@ -169,7 +182,7 @@
     for copy in to_smem:
         copy.wait()
 
-    arrive(5, 7, -5, -7, 8)
+    arrive(*(o for o in ARRIVE[3] if not BELOW[o]), *ARRIVE[4])
     for t in hand:
         t.wait_recv()
 
@@ -268,28 +281,22 @@
     for copy in lse_handed:
         copy.wait_recv()
 
-    half = lax.broadcasted_iota(jnp.int32, (1, WIDTH), 1) < ROWS
     wmat[...] = jnp.zeros((WIDTH, WIDTH), F32)
-
-    def where_is(d, r, k):
-        j = k * 32 + ((z + d) % NZ) * 2 + r
-        return ivec_s[0, 0, j], ivec_s[1, 0, j]
-
-    for d in range(NZ):
-        for k in range(3):
-            pair = []
-            for r in range(2):
-                i, n = where_is(d, r, k)
-                pair.append(jnp.where(n > 0, lses[i // 4, i % 4], NEG))
-            lrow[k, d] = jnp.where(half, pair[0], pair[1])[0]
-    l0, l1, l2 = lrow[0], lrow[1], lrow[2]
-    peak = jnp.maximum(jnp.maximum(l0, l1), l2)
-    w0, w1, w2 = jnp.exp(l0 - peak), jnp.exp(l1 - peak), jnp.exp(l2 - peak)
-    total = w0 + w1 + w2
+    away = lax.broadcasted_iota(jnp.int32, (NZ, WIDTH), 0)
+    half = lax.broadcasted_iota(jnp.int32, (NZ, WIDTH), 1) // ROWS
+    target = (((x * NZ + (z + away) % NZ) * NC + c) * 2 + half) * 4
+    ls = [jnp.full((NZ, WIDTH), NEG, F32) for _ in range(3)]
+    for gg in range(GROUPS):
+        for s in range(SLOTS):
+            here = rowtab[gg, s] - target
+            lse = lses[gg, s]
+            ls = [jnp.where(here == k, lse, ls[k]) for k in range(3)]
+    peak = jnp.maximum(jnp.maximum(ls[0], ls[1]), ls[2])
+    ws = [jnp.exp(l - peak) for l in ls]
+    total = ws[0] + ws[1] + ws[2]
     merged = peak + jnp.log(total)
-    wmat[0:16] = w0 / total
-    wmat[16:32] = w1 / total
-    wmat[32:48] = w2 / total
+    for k in range(3):
+        wmat[16 * k : 16 * (k + 1)] = ws[k] / total
     for d in range(NZ):
         clse[d] = merged[d : d + 1]
     wcol[...] = wmat[...].T
@@ -299,7 +306,7 @@
         for r in range(2):
             acc = jnp.zeros((ROWS, WIDTH), F32)
             for k in range(3):
-                i, _ = where_is(d, r, k)
+                i = ivec_s[0, k * 32 + ((z + d) % NZ) * 2 + r]
                 p = parts[i // 4, i % 4].reshape(ROWS, WIDTH).astype(F32)
                 acc = acc + wcol[r * ROWS : (r + 1) * ROWS, k * 16 + d : k * 16 + d + 1] * p
             cbuf[d, 4 * r : 4 * r + 4] = acc.astype(BF16).reshape(4, 16, WIDTH)
@@ -311,72 +318,89 @@
 
     up = {}
 
-    def send_up(o, data, lse):
+    def start_up(o, data, lse):
         i = PLACE[o]
         to = at(0, PARENT[o] - o, 0, 0)
         up[o] = (
+            send(lse, rlse.at[i], d_ss.at[i], d_rs.at[i], to),
             send(data, rbuf.at[i], c_ss.at[i], c_rs.at[i], to),
-            send(lse, rlse.at[i], d_ss.at[i], d_rs.at[i], to),
         )
+
+    for o in LEAVES:
+        build(-o)
+        start_up(o, cbuf.at[-o % NZ], clse.at[-o % NZ])
         for copy in up[o]:
             copy.start()
-
-    def gather_up(o):
-        for k in CHILDREN[o]:
-            for copy in up[k]:
-                copy.wait_recv()
-
-    for o in (5, 7, 8, -5, -7, 2, 4, -2, -4, 1, -1):
-        build(-o)
-        send_up(o, cbuf.at[-o % NZ], clse.at[-o % NZ])
-    for o in (6, -6, 3, -3, 0):
+    for o in (*HUBS, 0):
         build(-o)
     for copy in [*back, *lse_sent, *handed, *lse_handed]:
         copy.wait_send()
-    for n, o in enumerate((6, -6, 3, -3)):
-        gather_up(o)
-        ls = [clse[-o % NZ]] + [rlse[PLACE[k]] for k in CHILDREN[o]]
-        data = [cbuf[-o % NZ]] + [rbuf[PLACE[k]] for k in CHILDREN[o]]
-        peak = ls[0]
-        for l in ls[1:]:
-            peak = jnp.maximum(peak, l)
-        ws = [jnp.exp(l - peak) for l in ls]
-        total = ws[0]
-        for w in ws[1:]:
-            total = total + w
-        mlse[n] = peak + jnp.log(total)
-        for i, w in enumerate(ws):
-            wmat[i : i + 1] = w / total
-        wt = wmat[0:8].T
-        acc = jnp.zeros((WIDTH, WIDTH), F32)
-        for i, p in enumerate(data):
-            acc = acc + wt[:, i : i + 1] * p.reshape(WIDTH, WIDTH).astype(F32)
-        mbuf[n] = acc.astype(BF16).reshape(8, 16, WIDTH)
-        send_up(o, mbuf.at[n], mlse.at[n])
+
+    def merge(hubs):
+        columns = {}
+        for o in hubs:
+            for k in CHILDREN[o]:
+                up[k][0].wait_recv()
+            ls = [clse[-o % NZ]] + [rlse[PLACE[k]] for k in CHILDREN[o]]
+            peak = ls[0]
+            for l in ls[1:]:
+                peak = jnp.maximum(peak, l)
+            ws = [jnp.exp(l - peak) for l in ls]
+            total = ws[0]
+            for w in ws[1:]:
+                total = total + w
+            n = HUBS.index(o)
+            mlse[n] = peak + jnp.log(total)
+            start_up(o, mbuf.at[n], mlse.at[n])
+            up[o][0].start()
+            for i, w in enumerate(ws):
+                wmat[i : i + 1] = w / total
+            columns[o] = wmat[0:8].T
+        for o in hubs:
+            for k in CHILDREN[o]:
+                up[k][1].wait_recv()
+            data = [cbuf[-o % NZ]] + [rbuf[PLACE[k]] for k in CHILDREN[o]]
+            acc = jnp.zeros((WIDTH, WIDTH), F32)
+            for i, p in enumerate(data):
+                acc = acc + columns[o][:, i : i + 1] * p.reshape(WIDTH, WIDTH).astype(F32)
+            mbuf[HUBS.index(o)] = acc.astype(BF16).reshape(8, 16, WIDTH)
+            up[o][1].start()
+
+    for n in sorted({height(PARENT, o) for o in HUBS}):
+        merge([o for o in HUBS if height(PARENT, o) == n])
     for o in up:
-        if o not in (3, -3):
+        if PARENT[o] != 0:
             for copy in up[o]:
                 copy.wait_send()
-    gather_up(0)
+
+    for k in CHILDREN[0]:
+        up[k][0].wait_recv()
     for i, k in enumerate(CHILDREN[0]):
         wmat[i : i + 1] = rlse[PLACE[k]]
-    wmat[4:5] = clse[0]
+    wmat[len(CHILDREN[0]) : len(CHILDREN[0]) + 1] = clse[0]
     wt = wmat[0:8].T
-    done = []
+    ends = []
     for r in range(2):
         rs = slice(r * ROWS, (r + 1) * ROWS)
         tl = tail_lse[r][:, :1]
-        ls = [wt[rs, n : n + 1] for n in range(5)]
+        ls = [wt[rs, n : n + 1] for n in range(len(CHILDREN[0]) + 1)]
         peak = tl
         for l in ls:
             peak = jnp.maximum(peak, l)
         w = jnp.exp(tl - peak)
+        ws = [jnp.exp(l - peak) for l in ls]
         denom = w
-        acc = w * tail[r]
-        for n, ref in enumerate([rbuf.at[PLACE[k]] for k in CHILDREN[0]] + [cbuf.at[0]]):
-            w = jnp.exp(ls[n] - peak)
-            denom = denom + w
-            acc = acc + w * ref[4 * r : 4 * r + 4].reshape(ROWS, WIDTH).astype(F32)
+        for v in ws:
+            denom = denom + v
+        p = cbuf[0, 4 * r : 4 * r + 4].reshape(ROWS, WIDTH).astype(F32)
+        ends.append((ws, denom, w * tail[r] + ws[-1] * p))
+    for k in CHILDREN[0]:
+        up[k][1].wait_recv()
+    done = []
+    for r in range(2):
+        ws, denom, acc = ends[r]
+        for n, k in enumerate(CHILDREN[0]):
+            acc = acc + ws[n] * rbuf[PLACE[k], 4 * r : 4 * r + 4].reshape(ROWS, WIDTH).astype(F32)
         done.append(acc / denom)
     for a in range(4):
         heads = [
@@ -385,7 +409,7 @@
         ]
         out_ref[a] = jnp.concatenate(heads, axis=1).astype(BF16)
 
-    for o in (3, -3):
+    for o in CHILDREN[0]:
         for copy in up[o]:
             copy.wait_send()
 
@@ -410,23 +434,22 @@
             pltpu.VMEM((SLOTS, WIDTH, BLOCK), BF16),
             pltpu.VMEM((NZ, NC, 9, 16, WIDTH), BF16),
             pltpu.VMEM((GROUPS, SLOTS, 1, WIDTH), jnp.int32),
-            pltpu.VMEM((2, 1, WIDTH), jnp.int32),
+            pltpu.VMEM((1, WIDTH), jnp.int32),
             pltpu.SMEM((GROUPS, SLOTS, 1, WIDTH), jnp.int32),
-            pltpu.SMEM((2, 1, WIDTH), jnp.int32),
+            pltpu.SMEM((1, WIDTH), jnp.int32),
             pltpu.VMEM((3, 2, 9, 16, WIDTH), BF16),
             pltpu.VMEM((NX, 9, 16, WIDTH), BF16),
             pltpu.VMEM((NX, 9, 16, WIDTH), BF16),
             pltpu.VMEM((GROUPS, SLOTS, 4, 16, WIDTH), BF16),
             pltpu.VMEM((GROUPS, SLOTS, 1, WIDTH), F32),
-            pltpu.VMEM((3, NZ, WIDTH), F32),
             pltpu.VMEM((WIDTH, WIDTH), F32),
             pltpu.VMEM((WIDTH, WIDTH), F32),
             pltpu.VMEM((NZ, 8, 16, WIDTH), BF16),
             pltpu.VMEM((NZ, 1, WIDTH), F32),
             pltpu.VMEM((m, 8, 16, WIDTH), BF16),
             pltpu.VMEM((m, 1, WIDTH), F32),
-            pltpu.VMEM((4, 8, 16, WIDTH), BF16),
-            pltpu.VMEM((4, 1, WIDTH), F32),
+            pltpu.VMEM((len(HUBS), 8, 16, WIDTH), BF16),
+            pltpu.VMEM((len(HUBS), 1, WIDTH), F32),
             pltpu.VMEM((2, ROWS, WIDTH), F32),
             pltpu.VMEM((2, ROWS, WIDTH), F32),
             dma((5,)),

time: 62.2 us -> 61.4 us (0.987); the launches traced: 61.9 us -> 60.4 us
  Pallas kernels: 59.2 us -> 57.7 us
    pallas_call x1, Pallas kernels: 59.2 us -> 57.7 us  [shards(): pl.pallas_call(kernel, out_shape=jax.ShapeDtypeStruct(query.shape, BF16),...]
where the time goes in v5:
time: 61.4 us; the launch traced here: 60.4 us
  Pallas kernels  57.7 us (94%)
  local copies, waits for them, and re-layouts  1.4 us (2%)
  between operations  1.3 us (2%)
    pallas_call x1, Pallas kernels, shards(): pl.pallas_call(kernel, out_shape=jax.ShapeDtypeStruct(query.shape, BF16),...  57.7 us
    unnamed x1, local copies, waits for them, and re-layouts  1.4 us

profile of v5, /device:TPU:24, one launch (start us, length us, event | category | flops | bytes accessed | tf_op | source)
XLA Modules:
  0.0 60.4 jit_solution(911763161542787135)
XLA Ops:
  1.3 57.7 %lent_attention.1 = bf16[4,2,2048]{2,1,0:T(2,128)(2,1)} custom-call(bf16[4,2,2048]{2,1,0:T(2,128)(2,1)} %q_in.1, bf16[4,2,256]{2,1,0:T(2,128)(2,1)} %fresh_in.1, bf16[4,2048,256]{2,1,0:T(8,128)(2,1)} %kv_ref.1, s32[2]{0:T(128)} %len_in.1, s32[1]{0:T(128)S(6)} %copy.8.owner_in, s32[1]{0:T(128)S(6)} %copy.9.block_in), custom_call_target="tpu_custom_call" | custom-call | tf_op jit(solution)/shard_map/lent_attention/pallas_call | solution.py:421
  59.0 1.4 %copy.10 = bf16[4,2,2048]{2,1,0:T(2,128)(2,1)} copy(bf16[4,2,2048]{2,1,0:T(2,128)(2,1)} %lent_attention.1) | data formatting | bytes 65536

commit v6 on v5

--- a/solution.py
+++ b/solution.py
@@ -47,7 +47,7 @@
     kv, kt, qall, rowtab, ivec, tab_s, ivec_s, sel, got0, got1, parts, lses, wmat, wcol,
     cbuf, clse, rbuf, rlse, mbuf, mlse, tail, tail_lse,
     in_sem, kv_sem, sm_sem, y_ss, y_rs, t_ss, t_rs, w_ss, w_rs, a_ss, a_rs, h_ss, h_rs, s_ss, s_rs,
-    p_ss, p_rs, l_ss, l_rs, u_ss, u_rs, v_ss, v_rs, c_ss, c_rs, d_ss, d_rs,
+    p_ss, p_rs, l_ss, l_rs, u_ss, u_rs, c_ss, c_rs, d_ss, d_rs,
 ):
     me = lax.axis_index("inst")
     y = lax.axis_index("tp")
@@ -66,7 +66,8 @@
         )
 
     peers = [at(0, d, 0, 0) for d in NEAR]
-    peers += [at(dx, 0, 0, 0) for dx in X_PEERS] + [at(0, 0, 1, 0)]
+    row = [at(dx, 0, 0, 0) for dx in X_PEERS] + [at(0, 0, 1, 0)] + [at(dx, 0, 1, 0) for dx in X_PEERS]
+    peers += row
     peers += [at(0, 0, 0, d) for d in range(1, NY)]
     barrier = pltpu.get_barrier_semaphore()
     for p in peers:
@@ -89,11 +90,11 @@
         for r in range(2):
             tile = jnp.concatenate([qa[r : r + 1, WIDTH * h : WIDTH * (h + 1)] for h in range(16)], axis=0)
             q_ref[4 * r + a] = tile.astype(BF16)
-    row = lax.broadcasted_iota(jnp.int32, (16, WIDTH), 0) % 4
-    hi = jnp.where(row < 2, len_ref[0] // 64, len_ref[1] // 64)
-    lo = jnp.where(row < 2, len_ref[0] % 64, len_ref[1] % 64)
+    line = lax.broadcasted_iota(jnp.int32, (16, WIDTH), 0) % 4
+    hi = jnp.where(line < 2, len_ref[0] // 64, len_ref[1] // 64)
+    lo = jnp.where(line < 2, len_ref[0] % 64, len_ref[1] % 64)
     qall[z, c, 0:8] = q_ref[...]
-    qall[z, c, 8] = jnp.where(row % 2 == 0, hi, lo).astype(F32).astype(BF16)
+    qall[z, c, 8] = jnp.where(line % 2 == 0, hi, lo).astype(F32).astype(BF16)
     rowtab[g, y] = jnp.full((1, WIDTH), owner_ref[0] * 4 + block_ref[0], jnp.int32)
     pl.semaphore_wait(barrier, len(peers))
 
@@ -240,8 +241,7 @@
             lt = jnp.concatenate([lcols, lcols], axis=0).T
             for s in range(SLOTS):
                 lses[g, s] = lt[s : s + 1]
-            for i in range(4):
-                to = at(X_PEERS[i], 0, 0, 0) if i < 3 else at(0, 0, 1, 0)
+            for i, to in enumerate(row):
                 copy = send(lses.at[g], lses.at[g], l_ss.at[i], l_rs.at[i], to)
                 copy.start()
                 lse_sent.append(copy)
@@ -250,8 +250,7 @@
             part = jnp.dot(rounded[n], kv[s, :, WIDTH:], preferred_element_type=F32) / totals[n]
             parts[g, s] = part.astype(BF16).reshape(4, 16, WIDTH)
         mine = parts.at[g, 2 * half : 2 * half + 2]
-        for i in range(4):
-            to = at(X_PEERS[i], 0, 0, 0) if i < 3 else at(0, 0, 1, 0)
+        for i, to in enumerate(row if half else row[:4]):
             copy = send(mine, mine, p_ss.at[i, half], p_rs.at[i, half], to)
             copy.start()
             back.append(copy)
@@ -259,26 +258,13 @@
         copy.wait_send()
 
     handed = []
-
-    def hand_parts(half):
-        for i, dx in enumerate(X_PEERS):
-            back[half * 4 + i].wait_recv()
-            there = parts.at[((x - dx + NX) % NX) * NC + c, 2 * half : 2 * half + 2]
-            copy = send(there, there, u_ss.at[i, half], u_rs.at[i, half], at(0, 0, 1, 0))
-            copy.start()
-            handed.append(copy)
-
-    hand_parts(0)
-    lse_handed = []
     for i, dx in enumerate(X_PEERS):
-        lse_sent[i].wait_recv()
-        there = lses.at[((x - dx + NX) % NX) * NC + c]
-        copy = send(there, there, v_ss.at[i], v_rs.at[i], at(0, 0, 1, 0))
+        back[i].wait_recv()
+        there = parts.at[((x - dx + NX) % NX) * NC + c, 0:2]
+        copy = send(there, there, u_ss.at[i], u_rs.at[i], at(0, 0, 1, 0))
         copy.start()
-        lse_handed.append(copy)
-    hand_parts(1)
-    lse_sent[3].wait_recv()
-    for copy in lse_handed:
+        handed.append(copy)
+    for copy in lse_sent:
         copy.wait_recv()
 
     wmat[...] = jnp.zeros((WIDTH, WIDTH), F32)
@@ -311,9 +297,7 @@
                 acc = acc + wcol[r * ROWS : (r + 1) * ROWS, k * 16 + d : k * 16 + d + 1] * p
             cbuf[d, 4 * r : 4 * r + 4] = acc.astype(BF16).reshape(4, 16, WIDTH)
 
-    for half in range(2):
-        back[half * 4 + 3].wait_recv()
-    for copy in handed:
+    for copy in back[3:] + handed:
         copy.wait_recv()
 
     up = {}
@@ -326,14 +310,16 @@
             send(data, rbuf.at[i], c_ss.at[i], c_rs.at[i], to),
         )
 
-    for o in LEAVES:
+    now = [o for o in LEAVES if PARENT[o] != 0]
+    later = [o for o in LEAVES if o not in now]
+    for o in now:
         build(-o)
         start_up(o, cbuf.at[-o % NZ], clse.at[-o % NZ])
         for copy in up[o]:
             copy.start()
-    for o in (*HUBS, 0):
+    for o in (*HUBS, 0, *later):
         build(-o)
-    for copy in [*back, *lse_sent, *handed, *lse_handed]:
+    for copy in [*back, *lse_sent, *handed]:
         copy.wait_send()
 
     def merge(hubs):
@@ -368,6 +354,11 @@
 
     for n in sorted({height(PARENT, o) for o in HUBS}):
         merge([o for o in HUBS if height(PARENT, o) == n])
+        if n == 1:
+            for o in later:
+                start_up(o, cbuf.at[-o % NZ], clse.at[-o % NZ])
+                for copy in up[o]:
+                    copy.start()
     for o in up:
         if PARENT[o] != 0:
             for copy in up[o]:
@@ -461,9 +452,8 @@
             dma((m,)), dma((m,)),
             dma((m + 1,)), dma((m + 1,)),
             dma((3, 2)), dma((3, 2)),
-            dma((4, 2)), dma((4, 2)),
-            dma((4,)), dma((4,)),
-            dma((3, 2)), dma((3, 2)),
+            dma((7, 2)), dma((7, 2)),
+            dma((7,)), dma((7,)),
             dma((3,)), dma((3,)),
             dma((m,)), dma((m,)),
             dma((m,)), dma((m,)),

time: 61.4 us -> 61 us (level); the launches traced: 60.4 us -> 60.7 us
  no operation moved by 1% of the time
where the time goes in v6:
time: 61 us; the launch traced here: 60.7 us
  Pallas kernels  58 us (95%)
  local copies, waits for them, and re-layouts  1.4 us (2%)
  between operations  1.3 us (2%)
    pallas_call x1, Pallas kernels, shards(): pl.pallas_call(kernel, out_shape=jax.ShapeDtypeStruct(query.shape, BF16),...  58 us
    unnamed x1, local copies, waits for them, and re-layouts  1.4 us

profile of v6, /device:TPU:24, one launch (start us, length us, event | category | flops | bytes accessed | tf_op | source)
XLA Modules:
  0.0 60.7 jit_solution(11708914667333713682)
XLA Ops:
  1.3 58.0 %lent_attention.1 = bf16[4,2,2048]{2,1,0:T(2,128)(2,1)} custom-call(bf16[4,2,2048]{2,1,0:T(2,128)(2,1)} %q_in.1, bf16[4,2,256]{2,1,0:T(2,128)(2,1)} %fresh_in.1, bf16[4,2048,256]{2,1,0:T(8,128)(2,1)} %kv_ref.1, s32[2]{0:T(128)} %len_in.1, s32[1]{0:T(128)S(6)} %copy.8.owner_in, s32[1]{0:T(128)S(6)} %copy.9.block_in), custom_call_target="tpu_custom_call" | custom-call | tf_op jit(solution)/shard_map/lent_attention/pallas_call | solution.py:412
  59.3 1.4 %copy.10 = bf16[4,2,2048]{2,1,0:T(2,128)(2,1)} copy(bf16[4,2,2048]{2,1,0:T(2,128)(2,1)} %lent_attention.1) | data formatting | bytes 65536

commit v7 on v6

--- a/solution.py
+++ b/solution.py
@@ -249,11 +249,13 @@
             s = 2 * half + n
             part = jnp.dot(rounded[n], kv[s, :, WIDTH:], preferred_element_type=F32) / totals[n]
             parts[g, s] = part.astype(BF16).reshape(4, 16, WIDTH)
-        mine = parts.at[g, 2 * half : 2 * half + 2]
-        for i, to in enumerate(row if half else row[:4]):
-            copy = send(mine, mine, p_ss.at[i, half], p_rs.at[i, half], to)
-            copy.start()
-            back.append(copy)
+            if half == 0 and n == 0:
+                continue
+            mine = parts.at[g, s] if half else parts.at[g, 0:2]
+            for i, to in enumerate(row if half else row[:4]):
+                copy = send(mine, mine, p_ss.at[i, half * (n + 1)], p_rs.at[i, half * (n + 1)], to)
+                copy.start()
+                back.append(copy)
     for copy in [*spread.values(), *hand, *tables, *along_x, *across, *queries]:
         copy.wait_send()
 
@@ -452,7 +454,7 @@
             dma((m,)), dma((m,)),
             dma((m + 1,)), dma((m + 1,)),
             dma((3, 2)), dma((3, 2)),
-            dma((7, 2)), dma((7, 2)),
+            dma((7, 3)), dma((7, 3)),
             dma((7,)), dma((7,)),
             dma((3,)), dma((3,)),
             dma((m,)), dma((m,)),

time: 61 us -> 61 us (level)
  no operation moved by 1% of the time
where the time goes in v7:
time: 61 us; the launch traced here: 60.7 us
  Pallas kernels  58 us (95%)
  local copies, waits for them, and re-layouts  1.4 us (2%)
  between operations  1.3 us (2%)
    pallas_call x1, Pallas kernels, shards(): pl.pallas_call(kernel, out_shape=jax.ShapeDtypeStruct(query.shape, BF16),...  58 us
    unnamed x1, local copies, waits for them, and re-layouts  1.4 us

profile of v7, /device:TPU:24, one launch (start us, length us, event | category | flops | bytes accessed | tf_op | source)
XLA Modules:
  0.0 60.7 jit_solution(17713449362690599061)
XLA Ops:
  1.3 58.0 %lent_attention.1 = bf16[4,2,2048]{2,1,0:T(2,128)(2,1)} custom-call(bf16[4,2,2048]{2,1,0:T(2,128)(2,1)} %q_in.1, bf16[4,2,256]{2,1,0:T(2,128)(2,1)} %fresh_in.1, bf16[4,2048,256]{2,1,0:T(8,128)(2,1)} %kv_ref.1, s32[2]{0:T(128)} %len_in.1, s32[1]{0:T(128)S(6)} %copy.8.owner_in, s32[1]{0:T(128)S(6)} %copy.9.block_in), custom_call_target="tpu_custom_call" | custom-call | tf_op jit(solution)/shard_map/lent_attention/pallas_call | solution.py:414
  59.3 1.4 %copy.10 = bf16[4,2,2048]{2,1,0:T(2,128)(2,1)} copy(bf16[4,2,2048]{2,1,0:T(2,128)(2,1)} %lent_attention.1) | data formatting | bytes 65536
